TPU v7x, 512 devices: a whole 4x4x16 slice. The times are simulated.
512 devices in a mesh: owner: 64 (over z, y), local: 8 (over x, core).
Axes of the slice: x: 4, y: 4, z: 16, core: 2. Of those that a mesh axis runs over, the one named last changes fastest.
Arguments:
- vectors: bfloat16 [8, 1048576], P(None, ('owner', 'local')), may hold values from -6 to 6
- leaf_basis: bfloat16 [64, 1048576], P(None, ('owner', 'local')), may hold values from -0.75 to 0.75
- near_blocks: bfloat16 [4, 64, 1048576], P(None, None, ('owner', 'local')), may hold values from -0.375 to 0.375
- near_source: int32 [16384, 4], P(('owner', 'local')), may hold values from 0 to 16383, as said below
- up_transfer: bfloat16 [64, 1048576], P(None, ('owner', 'local')), may hold values from -0.375 to 0.375
- far_owner: int32 [4096, 8], P(('owner', 'local')), may hold values from 0 to 63, all different within a row; in each aligned block of 8 rows (0 to 7, 8 to 15, ...) at most 2 rows name the same one
- far_member: int32 [4096, 8], P(('owner', 'local')), may hold values from 0 to 63
- far_count: int32 [4096], P(('owner', 'local')), may hold values from 4 to 8
- far_blocks: bfloat16 [8, 64, 262144], P(None, None, ('owner', 'local')), may hold values from -0.25 to 0.25
- root_transfer: bfloat16 [64, 262144], P(None, ('owner', 'local')), may hold values from -0.26367188 to 0.26367188
- top_source: int32 [64, 16], P('owner', 'local'), may hold values from 0 to 63, all different within a row
- top_blocks: bfloat16 [16, 64, 4096], P('local', None, 'owner'), may hold values from -0.1875 to 0.1875
Outputs:
- product: bfloat16 [8, 1048576], P(None, ('owner', 'local'))
Inputs may be any that keep to these rules, and one draw needn't show every extreme that they name: `near_source`: slot 0 of each leaf's row is the leaf itself; every other slot names a leaf at most 4 leaves away from it. `far_owner`: each cluster's row names 8 different owners; among the 8 rows of one device no owner is named more than 2 times, a bound that some block reaches. `top_source`: each row names 16 different owners; every owner is named in some row.
All inputs are finite; a program needn't handle non-finite values.
Results may differ from a plain program's by a relative error of at most 0.009.
Values may be sent and summed in bfloat16 or wider, within the bound.
A program may use at most 64 MiB of HBM per device.

v0:
```python
import jax
import jax.numpy as jnp
from jax import lax
from jax.sharding import PartitionSpec as P

NV = 8
LEAF = 64
RANK = 64
CLUSTER_LEAVES = 4
NEAR = 4
REACH = 4
FAR = 8


def padded(block, sides, width):
    for axis, dim in sides:
        count = lax.axis_size(axis)
        forward = [(i, i + 1) for i in range(count - 1)]
        backward = [(target, source) for source, target in forward]
        low = lax.ppermute(
            lax.slice_in_dim(block, block.shape[dim] - width, None, axis=dim), axis, forward
        )
        high = lax.ppermute(lax.slice_in_dim(block, 0, width, axis=dim), axis, backward)
        block = jnp.concatenate([low, block, high], axis=dim)
    return block


def select_rows(piece, wanted):
    matches = (wanted[:, None] == jnp.arange(piece.shape[0], dtype=jnp.int32)[None, :]).astype(
        piece.dtype
    )
    return jnp.dot(matches, piece, preferred_element_type=jnp.float32)


def per_device(
    vectors,
    leaf_basis,
    near_blocks,
    near_source,
    up_transfer,
    far_owner,
    far_member,
    far_count,
    far_blocks,
    root_transfer,
    top_source,
    top_blocks,
):
    leaf_dev = leaf_basis.shape[1] // LEAF
    cluster_dev = leaf_dev // CLUSTER_LEAVES
    local_count = lax.axis_size("local")
    cluster_owner = cluster_dev * local_count
    skel_width = NV * RANK
    entries = cluster_dev * FAR
    extended = padded(vectors, ((("owner", "local"), 1),), REACH * LEAF)
    points = vectors.reshape(NV, leaf_dev, LEAF)
    basis = leaf_basis.reshape(RANK, leaf_dev, LEAF)
    leaf_skel = jnp.einsum(
        "vlp,klp->lvk", points, basis, preferred_element_type=jnp.float32
    ).astype(jnp.bfloat16)
    upward = up_transfer.reshape(RANK, cluster_dev, CLUSTER_LEAVES, RANK)
    cluster_skel = jnp.einsum(
        "tcvk,jtck->tvj",
        leaf_skel.reshape(cluster_dev, CLUSTER_LEAVES, NV, RANK),
        upward,
        preferred_element_type=jnp.float32,
    ).astype(jnp.bfloat16)
    flat_skel = cluster_skel.reshape(cluster_dev, skel_width)
    wanted = (far_owner * cluster_owner + far_member).reshape(entries)
    picked = select_rows(
        lax.all_gather(flat_skel, ("owner", "local"), axis=0, tiled=True), wanted
    ).astype(jnp.bfloat16)
    live = (jnp.arange(FAR, dtype=jnp.int32)[None, :] < far_count[:, None]).astype(jnp.bfloat16)
    picked = picked.reshape(cluster_dev, FAR, NV, RANK) * live[:, :, None, None]
    far_field = jnp.einsum(
        "tfvk,fjtk->tvj",
        picked,
        far_blocks.reshape(FAR, RANK, cluster_dev, RANK),
        preferred_element_type=jnp.float32,
    )
    rootward = root_transfer.reshape(RANK, cluster_dev, RANK)
    partial_root = jnp.einsum(
        "tvk,jtk->vj", cluster_skel, rootward, preferred_element_type=jnp.float32
    ).reshape(1, skel_width)
    own_root = lax.psum(partial_root, "local").astype(jnp.bfloat16)
    root_skel = lax.all_gather(own_root, "owner", axis=0, tiled=True)
    coupled = jnp.take(root_skel, top_source.reshape(-1), axis=0).reshape(-1, NV, RANK)
    top_share = jnp.einsum("svk,sjk->vj", coupled, top_blocks, preferred_element_type=jnp.float32)
    root_out = lax.psum(top_share, "local").astype(jnp.bfloat16)
    downward = jnp.einsum("vj,jtk->tvk", root_out, rootward, preferred_element_type=jnp.float32)
    cluster_out = (far_field + downward).astype(jnp.bfloat16)
    leaf_out = (
        jnp.einsum("tvj,jtck->tcvk", cluster_out, upward, preferred_element_type=jnp.float32)
        .reshape(leaf_dev, NV, RANK)
        .astype(jnp.bfloat16)
    )
    result = jnp.einsum("lvk,klp->vlp", leaf_out, basis, preferred_element_type=jnp.float32)
    device = lax.axis_index("owner") * local_count + lax.axis_index("local")
    near_position = near_source - device * leaf_dev + REACH
    beside_all = extended.reshape(NV, leaf_dev + 2 * REACH, LEAF)
    nearby = jnp.take(beside_all, near_position.T, axis=1)
    dense = near_blocks.reshape(NEAR, LEAF, leaf_dev, LEAF)
    result = result + jnp.einsum(
        "vjlp,jqlp->vlq", nearby, dense, preferred_element_type=jnp.float32
    )
    return result.reshape(NV, leaf_dev * LEAF).astype(jnp.bfloat16)


def solution(mesh):
    return jax.shard_map(
        per_device,
        mesh=mesh,
        in_specs=(
            P(None, ("owner", "local")),
            P(None, ("owner", "local")),
            P(None, None, ("owner", "local")),
            P(("owner", "local"), None),
            P(None, ("owner", "local")),
            P(("owner", "local"), None),
            P(("owner", "local"), None),
            P(("owner", "local")),
            P(None, None, ("owner", "local")),
            P(None, ("owner", "local")),
            P("owner", "local"),
            P("local", None, "owner"),
        ),
        out_specs=P(None, ("owner", "local")),
        check_vma=False,
    )
```

profile of v0, /device:TPU:1, one launch (start us, length us, event | category | flops | bytes accessed | tf_op | source)
XLA Modules:
  0.0 227.6 jit_solution(5584719174715672635)
XLA Ops:
  6.6 1.7 reshape.111
  8.3 0.9 reshape.110
  9.2 1.5 reshape.113
  10.7 0.4 convolution_convert_fusion.2
  11.0 0.3 fusion.8
  11.3 0.7 reshape.114
  12.1 4.5 %collective-permute-start = (bf16[8,256]{1,0:T(8,128)(2,1)S(1)}, bf16[8,256]{1,0:T(8,128)(2,1)S(1)}, u32[]{:S(2)}, u32[]{:S(2)}) collective-permute-start(bf16[8,256]{1,0:T(8,128)(2,1)S(1)} %get-tuple-element.7), channel_id=1, source_target_pairs={{0,1},{1,2},{2,3},{3,4},{4,5},{5,6},{6,7},{7,8},{8,9},{9,10},{10,1... | collective-permute-start | bytes 12296 | tf_op jit(solution)/shard_map/ppermute | solution.py:20
  16.6 5.6 %collective-permute-start.1 = (bf16[8,256]{1,0:T(8,128)(2,1)S(1)}, bf16[8,256]{1,0:T(8,128)(2,1)S(1)}, u32[]{:S(2)}, u32[]{:S(2)}) collective-permute-start(bf16[8,256]{1,0:T(8,128)(2,1)S(1)} %get-tuple-element.8), channel_id=1, source_target_pairs={{1,0},{2,1},{3,2},{4,3},{5,4},{6,5},{7,6},{8,7},{9,8},{10,9},{11,1... | collective-permute-start | bytes 12296 | tf_op jit(solution)/shard_map/ppermute | solution.py:23
  22.3 0.1 convolution_bitcast_fusion.4
  22.5 20.4 %psum.14 = bf16[1,512]{1,0:T(2,128)(2,1)S(1)} all-reduce(f32[1,512]{1,0:T(1,128)S(1)} %reshape.119), channel_id=1, replica_groups=mesh['owner'=64,'local'=8] {'local'}, use_global_device_ids=true, to_apply=%region_0.0 | all-reduce | flops 512 | bytes 3072 | tf_op jit(solution)/shard_map/psum | solution.py:85
  42.9 81.4 %all-gather = bf16[64,1,512]{2,1,0:T(2,128)(2,1)S(1)} all-gather(bf16[1,1,512]{2,1,0:T(2,128)(2,1)S(1)} %bitcast.68), channel_id=1, replica_groups=mesh['owner'=64,'local'=8] {'owner'}, dimensions={0}, use_global_device_ids=true | all-gather | bytes 66560 | tf_op jit(solution)/shard_map/all_gather | solution.py:86
  124.3 0.6 gather_fusion
  125.1 0.2 convolution_bitcast_fusion.3
  125.5 1.5 reshape.116
  127.0 3.3 %reshape.122 = bf16[4,64,32,64]{3,2,1,0:T(8,128)(2,1)S(1)} reshape(bf16[4,64,2048]{2,1,0:T(8,128)(2,1)} %param.14) | data formatting | bytes 2097152 | tf_op jit(solution)/shard_map/reshape | solution.py:102
  130.3 40.7 %psum.15 = bf16[8,64]{1,0:T(8,128)(2,1)S(1)} all-reduce(f32[8,64]{1,0:T(8,128)S(1)} %convolution_bitcast_fusion.3), channel_id=1, replica_groups=mesh['owner'=64,'local'=8] {'local'}, use_global_device_ids=true, to_apply=%region_1.2 | all-reduce | flops 512 | bytes 3072 | tf_op jit(solution)/shard_map/psum | solution.py:89
  171.2 1.4 gather_fusion.1
  172.5 2.0 fusion.2
  174.5 41.2 %all-gather.3.cloned.1.call-done = bf16[4096,512]{1,0:T(8,128)(2,1)} async-done(((bf16[8,512]{1,0:T(8,128)(2,1)}), bf16[4096,512]{1,0:T(8,128)(2,1)}) %all-gather.3.cloned.1.call-update) | async-done | bytes 4194320 | tf_op jit(solution)/shard_map/all_gather | solution.py:71
  215.7 3.1 %convolution_convert_fusion.1 = bf16[64,512]{1,0:T(8,128)(2,1)S(1)} fusion(bf16[4096,512]{1,0:T(8,128)(2,1)} %all-gather.3.cloned.1.call-done, s32[64]{0:T(128)S(1)} %eq.15), kind=kOutput, calls=%fused_computation.8 | convolution fusion | flops 268730368 | bytes 4260096 | tf_op jit(solution)/shard_map/dot_general | solution.py:32
  218.9 0.4 convolution_bitcast_fusion.1
  219.4 0.3 convolution_convert_fusion
  219.7 0.3 fusion.6
  220.0 0.7 convert_element_type.56
  (43 shorter events, 1.0 us)
Async XLA Ops:
  6.5 118.6 %copy-start = (bf16[2,64,64]{2,1,0:T(8,128)(2,1)S(1)}, bf16[2,64,64]{2,1,0:T(8,128)(2,1)}, u32[]{:S(2)}) copy-start(bf16[2,64,64]{2,1,0:T(8,128)(2,1)} %param.23) | copy-start | bytes 49156
  6.5 5.5 %copy-start.3 = (bf16[8,2048]{1,0:T(8,128)(2,1)S(1)}, bf16[8,2048]{1,0:T(8,128)(2,1)}, u32[]{:S(2)}) copy-start(bf16[8,2048]{1,0:T(8,128)(2,1)} %param.12) | copy-start | bytes 98308
  6.5 15.6 %copy-start.4 = (bf16[64,512]{1,0:T(8,128)(2,1)S(1)}, bf16[64,512]{1,0:T(8,128)(2,1)}, u32[]{:S(2)}) copy-start(bf16[64,512]{1,0:T(8,128)(2,1)} %param.21) | copy-start | bytes 196612
  6.5 117.8 %copy-start.9 = (s32[1,2]{1,0:T(1,128)S(1)}, s32[1,2]{1,0:T(1,128)}, u32[]{:S(2)}) copy-start(s32[1,2]{1,0:T(1,128)} %param.22) | copy-start | bytes 28
  6.5 118.5 %copy-start.7 = (s32[32,4]{0,1:T(4,128)S(1)}, s32[32,4]{0,1:T(4,128)}, u32[]{:S(2)}) copy-start(s32[32,4]{0,1:T(4,128)} %param.15) | copy-start | bytes 1540
  6.5 118.7 %copy-start.8 = (s32[8]{0:T(128)S(1)}, s32[8]{0:T(128)}, u32[]{:S(2)}) copy-start(s32[8]{0:T(128)} %param.19) | copy-start | bytes 100
  6.6 118.8 %copy-start.6 = (s32[8,8]{1,0:T(8,128)S(1)}, s32[8,8]{1,0:T(8,128)}, u32[]{:S(2)}) copy-start(s32[8,8]{1,0:T(8,128)} %param.17) | copy-start | bytes 772
  6.6 118.8 %copy-start.5 = (s32[8,8]{1,0:T(8,128)S(1)}, s32[8,8]{1,0:T(8,128)}, u32[]{:S(2)}) copy-start(s32[8,8]{1,0:T(8,128)} %param.18) | copy-start | bytes 772
  6.6 118.9 %copy-start.2 = (bf16[8,64,512]{2,1,0:T(8,128)(2,1)S(1)}, bf16[8,64,512]{2,1,0:T(8,128)(2,1)}, u32[]{:S(2)}) copy-start(bf16[8,64,512]{2,1,0:T(8,128)(2,1)} %param.20) | copy-start | bytes 1572868
  6.6 209.1 %all-gather.3.cloned.1.call-start = ((), (), s32[]{:S(2)}) async-start(), calls=%async_computation | async-start | bytes 4202496 | tf_op jit(solution)/shard_map/all_gather | solution.py:71
  12.1 158.9 %collective-permute-start = (bf16[8,256]{1,0:T(8,128)(2,1)S(1)}, bf16[8,256]{1,0:T(8,128)(2,1)S(1)}, u32[]{:S(2)}, u32[]{:S(2)}) collective-permute-start(bf16[8,256]{1,0:T(8,128)(2,1)S(1)} %get-tuple-element.7), channel_id=1, source_target_pairs={{0,1},{1,2},{2,3},{3,4},{4,5},{5,6},{6,7},{7,8},{8,9},{9,10},{10,1... | collective-permute-start | bytes 12296 | tf_op jit(solution)/shard_map/ppermute | solution.py:20
  16.6 154.4 %collective-permute-start.1 = (bf16[8,256]{1,0:T(8,128)(2,1)S(1)}, bf16[8,256]{1,0:T(8,128)(2,1)S(1)}, u32[]{:S(2)}, u32[]{:S(2)}) collective-permute-start(bf16[8,256]{1,0:T(8,128)(2,1)S(1)} %get-tuple-element.8), channel_id=1, source_target_pairs={{1,0},{2,1},{3,2},{4,3},{5,4},{6,5},{7,6},{8,7},{9,8},{10,9},{11,1... | collective-permute-start | bytes 12296 | tf_op jit(solution)/shard_map/ppermute | solution.py:23
  174.5 44.4 %copy-start.1 = (bf16[8,64,8,64]{3,2,1,0:T(8,128)(2,1)S(1)}, bf16[8,64,8,64]{3,2,1,0:T(8,128)(2,1)}, u32[]{:S(2)}) copy-start(bf16[8,64,8,64]{3,2,1,0:T(8,128)(2,1)} %reshape.116) | copy-start | bytes 1572868
Sparse Core Ops, SparseCore 0:
  12.2 203.5 all-gather.2
where the time goes:
time: 228 us
  blocking collectives  142 us (62%)
  waiting for transfers between devices  41.2 us (18%)
  between operations  13.6 us (6%)
  local copies, waits for them, and re-layouts  13 us (6%)
  starting transfers between devices  10.1 us (4%)
  matrix products  7.05 us (3%)
    all_gather x1, blocking collectives, per_device(): root_skel = lax.all_gather(own_root, 'owner', axis=0, tiled=True)  81.4 us
    all_gather x1, waiting for transfers between devices, per_device(): lax.all_gather(flat_skel, ('owner', 'local'), axis=0, tiled=True)  41.2 us
    psum x1, blocking collectives, per_device(): root_out = lax.psum(top_share, 'local').astype(jnp.bfloat16)  40.7 us
    psum x1, blocking collectives, per_device(): own_root = lax.psum(partial_root, 'local').astype(jnp.bfloat16)  20.4 us
    ppermute x1, starting transfers between devices, padded(): lax.ppermute(lax.slice_in_dim(block, 0, width, axis=dim), axis, backward)  5.57 us
  transfers between devices with their start and end apart: 3, of which 1 were waited for; matrix products, arithmetic and copies ran while one was open for 4% of the time, Pallas kernels for 0%

commit v1 on v0

v1 whole, which is shorter than its diff:
```python
import functools

import jax
import jax.numpy as jnp
from jax import lax
from jax.experimental import pallas as pl
from jax.experimental.pallas import tpu as pltpu
from jax.sharding import PartitionSpec as P

MESH = pl.DeviceIdType.MESH
NV = 8
LEAF = 64
RANK = 64
CLUSTER_LEAVES = 4
REACH = 4
HALF = 64
WIDE = 128
QUAD = 256


def dot(left, right):
    return jnp.dot(left, right, preferred_element_type=jnp.float32)


def dot_t(left, right):
    return lax.dot_general(left, right, (((1,), (1,)), ((), ())), preferred_element_type=jnp.float32)


def wait_bytes(ref, sem):
    pltpu.make_async_copy(ref, ref, sem).wait()


def kernel(
    owners,
    locals_,
    vec,
    basis,
    near,
    up,
    far,
    root_t,
    top_b,
    near_src,
    owner_s,
    count_s,
    owner_v,
    member_v,
    top_src,
    out,
    vec_b,
    basis_b,
    near_b,
    up_b,
    far_b,
    root_b,
    topb_b,
    load_sem,
    pair_basis,
    ext,
    near_res,
    rank_b,
    rank_s,
    halo,
    req_row,
    req,
    req_s,
    tops_row,
    tops,
    tops_s,
    topw,
    skel,
    part,
    root_tile,
    roots,
    far_send,
    far_recv,
    share,
    smem_sem,
    send_sem,
    recv_sem,
):
    o, l = lax.axis_index("owner"), lax.axis_index("local")
    me = o * locals_ + l
    total = owners * locals_
    clusters = skel.shape[0] // locals_
    slots = far_b.shape[0]
    near_slots = near_b.shape[0]
    leaves = clusters * CLUSTER_LEAVES
    pairs = leaves // 2
    rounds = owners // locals_
    left, right = lax.rem(me + total - 1, total), lax.rem(me + 1, total)
    left_id = (left // locals_, lax.rem(left, locals_))
    right_id = (right // locals_, lax.rem(right, locals_))
    HALO, REQ, TOPS, TOPW, SKEL, PART, ROOT, FARS, SHARE, HALO2 = range(10)

    def load(i, source, target):
        copy = pltpu.make_async_copy(source, target, load_sem.at[i])
        copy.start()
        return copy

    load_vec = load(0, vec, vec_b)
    load_basis = load(1, basis, basis_b)
    load_up = load(2, up, up_b)
    load_root = load(3, root_t, root_b)
    load_topb = load(4, top_b, topb_b)
    load_near = load(5, near, near_b)
    load_far = load(6, far, far_b)

    def remote(source, target, kind, device):
        return pltpu.make_async_remote_copy(
            src_ref=source,
            dst_ref=target,
            send_sem=send_sem.at[kind],
            recv_sem=recv_sem.at[kind],
            device_id=device,
            device_id_type=MESH,
        )

    barrier = pltpu.get_barrier_semaphore()

    def greet(device):
        pl.semaphore_signal(barrier, inc=1, device_id=device, device_id_type=MESH)

    @pl.loop(1, locals_)
    def _(d):
        greet((o, lax.rem(l + d, locals_)))

    greet(left_id)
    greet(right_id)

    @pl.loop(1, owners)
    def _(d):
        greet((lax.rem(o + d, owners), l))

    lane = lax.broadcasted_iota(jnp.int32, (1, WIDE), 1)
    lanes = lax.broadcasted_iota(jnp.int32, (clusters, WIDE), 1)
    key = jnp.where(lanes >= HALF, lanes - HALF, lanes)
    named = jnp.zeros((clusters, WIDE), jnp.int32)
    member = jnp.zeros((clusters, WIDE), jnp.int32)
    for f in range(slots):
        same = owner_v[:, f : f + 1] == key
        named = jnp.where(same, 1, named)
        member = jnp.where(same, member_v[:, f : f + 1], member)
    second = (lane >= HALF).astype(jnp.int32)
    run = jnp.zeros((1, WIDE), jnp.int32)
    wanted = jnp.zeros((1, WIDE), jnp.int32)
    for t in range(clusters):
        rank_b[t : t + 1, :] = run
        wanted = jnp.where(run == second, wanted + member[t : t + 1], wanted)
        run = run + named[t : t + 1]
    req_row[...] = wanted
    req[pl.ds(o, 1), :, :] = wanted.reshape(1, 1, WIDE)
    rank_copy = pltpu.make_async_copy(rank_b, rank_s, smem_sem.at[0])
    rank_copy.start()
    tops_row[...] = jnp.zeros((1, WIDE), jnp.int32)
    tops_row[:, 0:2] = top_src[...]
    tops[pl.ds(l, 1), :, :] = tops_row[...].reshape(1, 1, WIDE)

    low = lax.broadcasted_iota(jnp.int32, (NV, WIDE), 1) < HALF
    low_ones = (lax.broadcasted_iota(jnp.int32, (RANK, WIDE), 1) < HALF).astype(jnp.bfloat16)
    high_ones = (lax.broadcasted_iota(jnp.int32, (RANK, WIDE), 1) >= HALF).astype(jnp.bfloat16)
    load_vec.wait()
    load_basis.wait()
    load_up.wait()
    first = l * clusters
    tiles = []
    for t in range(clusters):
        parts = []
        for q in (2 * t, 2 * t + 1):
            block = basis_b[:, q * WIDE : (q + 1) * WIDE]
            diagonal = jnp.concatenate([block * low_ones, block * high_ones], axis=0)
            pair_basis[q] = diagonal
            parts.append(dot_t(vec_b[:, q * WIDE : (q + 1) * WIDE], diagonal))
        leaf_skel = jnp.concatenate(parts, axis=1).astype(jnp.bfloat16)
        block = up_b[:, t * QUAD : (t + 1) * QUAD]
        tile = dot_t(leaf_skel, jnp.concatenate([block, block], axis=0)).astype(jnp.bfloat16)
        skel[pl.ds(first + t, 1), :, :] = tile.reshape(1, NV, WIDE)
        tiles.append(tile.astype(jnp.float32))
    load_root.wait()
    rows = jnp.concatenate(
        [jnp.where(low, tiles[2 * q], tiles[2 * q + 1]) for q in range(clusters // 2)], axis=1
    ).astype(jnp.bfloat16)
    rootward = root_b[...]
    part[pl.ds(l, 1), :, :] = dot_t(rows, jnp.concatenate([rootward, rootward], axis=0)).reshape(1, NV, WIDE)

    load_topb.wait()
    topw[pl.ds(l, 1), :, :] = jnp.concatenate([topb_b[0], topb_b[1]], axis=1).reshape(1, RANK, WIDE)

    pl.semaphore_wait(barrier, owners - 1 + locals_ - 1 + 2)

    @pl.loop(1, locals_)
    def _(d):
        peer = (o, lax.rem(l + d, locals_))
        own = skel.at[pl.ds(first, clusters)]
        remote(own, own, SKEL, peer).start()
        mine = part.at[pl.ds(l, 1)]
        remote(mine, mine, PART, peer).start()

    @pl.loop(1, owners)
    def _(d):
        target = req.at[pl.ds(o, 1)]
        remote(target, target, REQ, (lax.rem(o + d, owners), l)).start()

    @pl.loop(1, locals_)
    def _(d):
        peer = (o, lax.rem(l + d, locals_))
        mine = tops.at[pl.ds(l, 1)]
        remote(mine, mine, TOPS, peer).start()
        block = topw.at[pl.ds(l, 1)]
        remote(block, block, TOPW, peer).start()

    edge = REACH * LEAF
    width = leaves * LEAF
    remote(vec_b.at[:, pl.ds(width - edge, edge)], halo.at[0], HALO, right_id).start()
    remote(vec_b.at[:, pl.ds(0, edge)], halo.at[1], HALO2, left_id).start()

    wait_bytes(part.at[pl.ds(0, locals_ - 1)], recv_sem.at[PART])
    root = part[0]
    for other in range(1, locals_):
        root = root + part[other]
    root_tile[...] = root.astype(jnp.bfloat16)

    @pl.when(l == 0)
    def _():
        roots[0] = root_tile[...]

    @pl.when(l != 0)
    def _():
        remote(root_tile, roots.at[0], ROOT, (lax.rem(o + l, owners), l)).start()

    @pl.loop(1, rounds)
    def _(i):
        remote(root_tile, roots.at[i], ROOT, (lax.rem(o + l + locals_ * i, owners), l)).start()

    wait_bytes(req.at[pl.ds(0, owners - 1)], recv_sem.at[REQ])
    req_copy = pltpu.make_async_copy(req, req_s, smem_sem.at[1])
    req_copy.start()
    wait_bytes(skel.at[pl.ds(0, clusters * (locals_ - 1))], recv_sem.at[SKEL])
    req_copy.wait()

    def chosen(asker):
        a = skel[req_s[asker, 0, o]].astype(jnp.float32)
        b = skel[req_s[asker, 0, HALF + o]].astype(jnp.float32)
        return jnp.where(low, a, b).astype(jnp.bfloat16).reshape(1, NV, WIDE)

    far_recv[pl.ds(o, 1), :, :] = chosen(o)

    @pl.loop(1, owners)
    def _(d):
        asker = lax.rem(o + d, owners)
        far_send[pl.ds(asker, 1), :, :] = chosen(asker)
        remote(far_send.at[pl.ds(asker, 1)], far_recv.at[pl.ds(o, 1)], FARS, (asker, l)).start()

    wait_bytes(tops.at[pl.ds(0, locals_ - 1)], recv_sem.at[TOPS])
    tops_copy = pltpu.make_async_copy(tops, tops_s, smem_sem.at[2])
    tops_copy.start()
    wait_bytes(topw.at[pl.ds(0, locals_ - 1)], recv_sem.at[TOPW])
    tops_copy.wait()

    @pl.when(l == 0)
    def _():
        wait_bytes(roots.at[pl.ds(0, rounds - 1)], recv_sem.at[ROOT])

    @pl.when(l != 0)
    def _():
        wait_bytes(roots, recv_sem.at[ROOT])

    def coupled(s):
        away = lax.rem(o - l - tops_s[s // 2, 0, s % 2] + 2 * owners, owners)
        tile = roots[away // locals_].astype(jnp.float32)
        return jnp.where(lax.rem(away, locals_) == 0, tile, 0.0)

    total_share = jnp.zeros((NV, WIDE), jnp.float32)
    for other in range(locals_):
        lhs = jnp.where(low, coupled(2 * other), coupled(2 * other + 1)).astype(jnp.bfloat16)
        block = topw[other]
        total_share = total_share + dot_t(lhs, jnp.concatenate([block, block], axis=0))
    share[pl.ds(l, 1), :, :] = total_share.reshape(1, NV, WIDE)

    @pl.loop(1, locals_)
    def _(d):
        mine = share.at[pl.ds(l, 1)]
        remote(mine, mine, SHARE, (o, lax.rem(l + d, locals_))).start()

    wait_bytes(halo.at[0], recv_sem.at[HALO])
    wait_bytes(halo.at[1], recv_sem.at[HALO2])

    def spread(pair, at):
        pair = pair.astype(jnp.float32)
        turned = pltpu.roll(pair, HALF, 1)
        ext[at] = jnp.where(low, pair, turned)
        ext[at + 1] = jnp.where(low, turned, pair)

    for q in range(REACH // 2):
        spread(halo[0, :, q * WIDE : (q + 1) * WIDE], 2 * q)
        spread(halo[1, :, q * WIDE : (q + 1) * WIDE], REACH + leaves + 2 * q)
    for q in range(pairs):
        spread(vec_b[:, q * WIDE : (q + 1) * WIDE], REACH + 2 * q)
    load_near.wait()
    zero = jnp.zeros((NV, WIDE), jnp.float32)

    def quad(pieces):
        rows = [
            jnp.concatenate([jnp.where(low, pieces[0], 0.0), zero], axis=1),
            jnp.concatenate([jnp.where(low, 0.0, pieces[1]), zero], axis=1),
            jnp.concatenate([zero, jnp.where(low, pieces[2], 0.0)], axis=1),
            jnp.concatenate([zero, jnp.where(low, 0.0, pieces[3])], axis=1),
        ]
        return jnp.concatenate(rows, axis=0).astype(jnp.bfloat16)

    offset = REACH - me * leaves

    def inside(at):
        return jnp.minimum(jnp.maximum(at, 0), leaves + 2 * REACH - 1)

    for t in range(clusters):
        acc = jnp.zeros((CLUSTER_LEAVES * NV, LEAF), jnp.float32)
        for i in range(near_slots):
            lhs = quad([ext[inside(near_src[i, CLUSTER_LEAVES * t + c] + offset)] for c in range(CLUSTER_LEAVES)])
            acc = acc + dot_t(lhs, near_b[i, :, t * QUAD : (t + 1) * QUAD])
        for c in range(0, CLUSTER_LEAVES, 2):
            near_res[2 * t + c // 2] = jnp.concatenate(
                [acc[c * NV : (c + 1) * NV], acc[(c + 1) * NV : (c + 2) * NV]], axis=1
            )

    wait_bytes(share.at[pl.ds(0, locals_ - 1)], recv_sem.at[SHARE])
    summed = share[0]
    for other in range(1, locals_):
        summed = summed + share[other]
    root_out = summed[:, 0:RANK].astype(jnp.bfloat16)
    downward = dot(root_out, root_b[...])
    rank_copy.wait()
    load_far.wait()

    wait_bytes(far_recv.at[pl.ds(0, owners - 1)], recv_sem.at[FARS])

    def picked(t, f):
        source = owner_s[t, f]
        tile = far_recv[source].astype(jnp.float32)
        tile = jnp.where(rank_s[t, source] == t % 2, tile, pltpu.roll(tile, HALF, 1))
        return jnp.where(f < count_s[t], tile, 0.0)

    for g in range(clusters // 4):
        acc = jnp.zeros((4 * NV, RANK), jnp.float32)
        for f in range(slots):
            lhs = quad([picked(4 * g + t, f) for t in range(4)])
            acc = acc + dot_t(lhs, far_b[f, :, g * QUAD : (g + 1) * QUAD])
        for t in range(4):
            at = 4 * g + t
            cluster_out = acc[t * NV : (t + 1) * NV] + downward[:, at * RANK : (at + 1) * RANK]
            leaf_out = dot(cluster_out.astype(jnp.bfloat16), up_b[:, at * QUAD : (at + 1) * QUAD]).astype(jnp.bfloat16)
            for c in range(2):
                q = 2 * at + c
                result = dot(leaf_out[:, c * WIDE : (c + 1) * WIDE], pair_basis[q]) + near_res[q]
                out[:, q * WIDE : (q + 1) * WIDE] = result.astype(jnp.bfloat16)

    wait_bytes(skel.at[pl.ds(0, clusters * (locals_ - 1))], send_sem.at[SKEL])
    wait_bytes(part.at[pl.ds(0, locals_ - 1)], send_sem.at[PART])
    wait_bytes(req.at[pl.ds(0, owners - 1)], send_sem.at[REQ])
    wait_bytes(tops.at[pl.ds(0, locals_ - 1)], send_sem.at[TOPS])
    wait_bytes(topw.at[pl.ds(0, locals_ - 1)], send_sem.at[TOPW])
    wait_bytes(halo.at[0], send_sem.at[HALO])
    wait_bytes(halo.at[1], send_sem.at[HALO2])

    @pl.when(l == 0)
    def _():
        wait_bytes(roots.at[pl.ds(0, rounds - 1)], send_sem.at[ROOT])

    @pl.when(l != 0)
    def _():
        wait_bytes(roots, send_sem.at[ROOT])

    wait_bytes(share.at[pl.ds(0, locals_ - 1)], send_sem.at[SHARE])
    wait_bytes(far_recv.at[pl.ds(0, owners - 1)], send_sem.at[FARS])


def per_device(
    owners,
    locals_,
    vectors,
    leaf_basis,
    near_blocks,
    near_source,
    up_transfer,
    far_owner,
    far_member,
    far_count,
    far_blocks,
    root_transfer,
    top_source,
    top_blocks,
):
    clusters = far_owner.shape[0]
    leaves = clusters * CLUSTER_LEAVES
    bf16, f32, i32 = jnp.bfloat16, jnp.float32, jnp.int32
    hbm = pl.BlockSpec(memory_space=pl.ANY)
    smem = pl.BlockSpec(memory_space=pltpu.SMEM)
    vmem = pl.BlockSpec(memory_space=pltpu.VMEM)
    big = (vectors, leaf_basis, near_blocks, up_transfer, far_blocks, root_transfer, top_blocks)
    return pl.pallas_call(
        functools.partial(kernel, owners, locals_),
        out_shape=jax.ShapeDtypeStruct(vectors.shape, bf16),
        in_specs=[hbm] * 7 + [smem] * 3 + [vmem] * 3,
        out_specs=vmem,
        scratch_shapes=[pltpu.VMEM(a.shape, bf16) for a in big]
        + [
            pltpu.SemaphoreType.DMA((7,)),
            pltpu.VMEM((leaves // 2, WIDE, WIDE), bf16),
            pltpu.VMEM((leaves + 2 * REACH, NV, WIDE), f32),
            pltpu.VMEM((leaves // 2, NV, WIDE), f32),
            pltpu.VMEM((clusters, WIDE), i32),
            pltpu.SMEM((clusters, WIDE), i32),
            pltpu.VMEM((2, NV, REACH * LEAF), bf16),
            pltpu.VMEM((1, WIDE), i32),
            pltpu.VMEM((owners, 1, WIDE), i32),
            pltpu.SMEM((owners, 1, WIDE), i32),
            pltpu.VMEM((1, WIDE), i32),
            pltpu.VMEM((locals_, 1, WIDE), i32),
            pltpu.SMEM((locals_, 1, WIDE), i32),
            pltpu.VMEM((locals_, RANK, WIDE), bf16),
            pltpu.VMEM((clusters * locals_, NV, WIDE), bf16),
            pltpu.VMEM((locals_, NV, WIDE), f32),
            pltpu.VMEM((NV, WIDE), bf16),
            pltpu.VMEM((owners // locals_, NV, WIDE), bf16),
            pltpu.VMEM((owners, NV, WIDE), bf16),
            pltpu.VMEM((owners, NV, WIDE), bf16),
            pltpu.VMEM((locals_, NV, WIDE), f32),
            pltpu.SemaphoreType.DMA((3,)),
            pltpu.SemaphoreType.DMA((10,)),
            pltpu.SemaphoreType.DMA((10,)),
        ],
        compiler_params=pltpu.CompilerParams(
            collective_id=0, has_side_effects=True, vmem_limit_bytes=32 * 1024 * 1024
        ),
    )(*big, near_source.T, far_owner, far_count, far_owner, far_member, top_source)


def solution(mesh):
    return jax.shard_map(
        functools.partial(per_device, mesh.shape["owner"], mesh.shape["local"]),
        mesh=mesh,
        in_specs=(
            P(None, ("owner", "local")),
            P(None, ("owner", "local")),
            P(None, None, ("owner", "local")),
            P(("owner", "local"), None),
            P(None, ("owner", "local")),
            P(("owner", "local"), None),
            P(("owner", "local"), None),
            P(("owner", "local")),
            P(None, None, ("owner", "local")),
            P(None, ("owner", "local")),
            P("owner", "local"),
            P("local", None, "owner"),
        ),
        out_specs=P(None, ("owner", "local")),
        check_vma=False,
    )
```

time: 228 us -> 52.3 us (0.23)
  the two profiles are of different devices: /device:TPU:1 before, /device:TPU:4 now
where the time goes in v1:
time: 52.3 us; the launch traced here: 51.7 us
  Pallas kernels  41.9 us (80%)
  local copies, waits for them, and re-layouts  9.86 us (19%)
    pallas_call x1, Pallas kernels, per_device(): pl.pallas_call(functools.partial(kernel, owners, locals_), out_shape=jax....  41.9 us
    unnamed x25, local copies, waits for them, and re-layouts  9.86 us

profile of v1, /device:TPU:4, one launch (start us, length us, event | category | flops | bytes accessed | tf_op | source)
XLA Modules:
  0.0 51.7 jit_solution(8086813272571295922)
XLA Ops:
  0.0 0.0 copy-start.11
  0.0 0.0 copy-start.10
  0.0 0.7 %copy-done.11 = s32[1,2]{1,0:T(1,128)S(1)} copy-done((s32[1,2]{1,0:T(1,128)S(1)}, s32[1,2]{1,0:T(1,128)}, u32[]{:S(2)}) %copy-start.11) | copy-done | bytes 32
  0.7 0.0 copy-done.10
  0.7 0.0 copy-start
  0.7 1.2 %copy-done = bf16[4,64,2048]{2,1,0:T(8,128)(2,1)S(1)} copy-done((bf16[4,64,2048]{2,1,0:T(8,128)(2,1)S(1)}, bf16[4,64,2048]{2,1,0:T(8,128)(2,1)}, u32[]{:S(2)}) %copy-start) | copy-done | bytes 1048600
  1.9 0.0 copy-start.1
  1.9 1.0 %copy-done.1 = bf16[8,64,512]{2,1,0:T(8,128)(2,1)S(1)} copy-done((bf16[8,64,512]{2,1,0:T(8,128)(2,1)S(1)}, bf16[8,64,512]{2,1,0:T(8,128)(2,1)}, u32[]{:S(2)}) %copy-start.1) | copy-done | bytes 524312
  2.9 0.0 copy-start.2
  2.9 0.9 %copy-done.2 = bf16[64,2048]{1,0:T(8,128)(2,1)S(1)} copy-done((bf16[64,2048]{1,0:T(8,128)(2,1)S(1)}, bf16[64,2048]{1,0:T(8,128)(2,1)}, u32[]{:S(2)}) %copy-start.2) | copy-done | bytes 262168
  3.9 0.0 copy-start.3
  3.9 0.9 %copy-done.3 = bf16[64,2048]{1,0:T(8,128)(2,1)S(1)} copy-done((bf16[64,2048]{1,0:T(8,128)(2,1)S(1)}, bf16[64,2048]{1,0:T(8,128)(2,1)}, u32[]{:S(2)}) %copy-start.3) | copy-done | bytes 262168
  4.8 0.0 copy-start.4
  4.8 0.8 %copy-done.4 = bf16[64,512]{1,0:T(8,128)(2,1)S(1)} copy-done((bf16[64,512]{1,0:T(8,128)(2,1)S(1)}, bf16[64,512]{1,0:T(8,128)(2,1)}, u32[]{:S(2)}) %copy-start.4) | copy-done | bytes 65560
  5.7 0.0 copy-start.5
  5.7 0.8 %copy-done.5 = bf16[8,2048]{1,0:T(8,128)(2,1)S(1)} copy-done((bf16[8,2048]{1,0:T(8,128)(2,1)S(1)}, bf16[8,2048]{1,0:T(8,128)(2,1)}, u32[]{:S(2)}) %copy-start.5) | copy-done | bytes 32792
  6.4 0.8 %copy-done.6 = bf16[2,64,64]{2,1,0:T(8,128)(2,1)S(1)} copy-done((bf16[2,64,64]{2,1,0:T(8,128)(2,1)S(1)}, bf16[2,64,64]{2,1,0:T(8,128)(2,1)}, u32[]{:S(2)}) %copy-start.6) | copy-done | bytes 16408
  7.2 0.0 copy-start.7
  7.2 0.7 %copy-done.7 = s32[8,8]{1,0:T(8,128)S(1)} copy-done((s32[8,8]{1,0:T(8,128)S(1)}, s32[8,8]{1,0:T(8,128)}, u32[]{:S(2)}) %copy-start.7) | copy-done | bytes 280
  7.9 0.0 copy-start.8
  7.9 0.7 %copy-done.8 = s32[8,8]{1,0:T(8,128)S(1)} copy-done((s32[8,8]{1,0:T(8,128)S(1)}, s32[8,8]{1,0:T(8,128)}, u32[]{:S(2)}) %copy-start.8) | copy-done | bytes 280
  8.6 0.7 %copy-done.9 = s32[32,4]{0,1:T(4,128)S(1)} copy-done((s32[32,4]{0,1:T(4,128)S(1)}, s32[32,4]{0,1:T(4,128)}, u32[]{:S(2)}) %copy-start.9) | copy-done | bytes 536
  9.3 41.9 %shard_map.118 = bf16[8,2048]{1,0:T(8,128)(2,1)S(1)} custom-call(bf16[8,2048]{1,0:T(8,128)(2,1)S(1)} %copy-done.5, bf16[64,2048]{1,0:T(8,128)(2,1)S(1)} %copy-done.2, bf16[4,64,2048]{2,1,0:T(8,128)(2,1)S(1)} %copy-done, bf16[64,2048]{1,0:T(8,128)(2,1)S(1)} %copy-done.3, bf16[8,64,512]{2,1,0:T(8,128)(2,1)S(1)} %copy-done.1, bf16[64,512]{1,0:T(8,128)(2,1)S(1)} %copy-done.4, ...), custom_call_target="tpu_custom_call" | custom-call | tf_op jit(solution)/shard_map/pallas_call | solution.py:400
  51.1 0.6 %copy.14 = bf16[8,2048]{1,0:T(8,128)(2,1)} copy(bf16[8,2048]{1,0:T(8,128)(2,1)S(1)} %shard_map.118) | data formatting | bytes 65536
  (2 shorter events, 0.0 us)
Async XLA Ops:
  0.0 0.7 %copy-start.11 = (s32[1,2]{1,0:T(1,128)S(1)}, s32[1,2]{1,0:T(1,128)}, u32[]{:S(2)}) copy-start(s32[1,2]{1,0:T(1,128)} %top_src.1) | copy-start | bytes 28
  0.0 0.7 %copy-start.10 = (s32[8]{0:T(128)S(1)}, s32[8]{0:T(128)}, u32[]{:S(2)}) copy-start(s32[8]{0:T(128)} %count_s.1) | copy-start | bytes 100
  0.7 1.2 %copy-start = (bf16[4,64,2048]{2,1,0:T(8,128)(2,1)S(1)}, bf16[4,64,2048]{2,1,0:T(8,128)(2,1)}, u32[]{:S(2)}) copy-start(bf16[4,64,2048]{2,1,0:T(8,128)(2,1)} %near.1) | copy-start | bytes 3145732
  1.9 1.0 %copy-start.1 = (bf16[8,64,512]{2,1,0:T(8,128)(2,1)S(1)}, bf16[8,64,512]{2,1,0:T(8,128)(2,1)}, u32[]{:S(2)}) copy-start(bf16[8,64,512]{2,1,0:T(8,128)(2,1)} %far.1) | copy-start | bytes 1572868
  2.9 0.9 %copy-start.2 = (bf16[64,2048]{1,0:T(8,128)(2,1)S(1)}, bf16[64,2048]{1,0:T(8,128)(2,1)}, u32[]{:S(2)}) copy-start(bf16[64,2048]{1,0:T(8,128)(2,1)} %basis.1) | copy-start | bytes 786436
  3.9 0.9 %copy-start.3 = (bf16[64,2048]{1,0:T(8,128)(2,1)S(1)}, bf16[64,2048]{1,0:T(8,128)(2,1)}, u32[]{:S(2)}) copy-start(bf16[64,2048]{1,0:T(8,128)(2,1)} %up.1) | copy-start | bytes 786436
  4.8 0.8 %copy-start.4 = (bf16[64,512]{1,0:T(8,128)(2,1)S(1)}, bf16[64,512]{1,0:T(8,128)(2,1)}, u32[]{:S(2)}) copy-start(bf16[64,512]{1,0:T(8,128)(2,1)} %root_t.1) | copy-start | bytes 196612
  5.7 0.8 %copy-start.5 = (bf16[8,2048]{1,0:T(8,128)(2,1)S(1)}, bf16[8,2048]{1,0:T(8,128)(2,1)}, u32[]{:S(2)}) copy-start(bf16[8,2048]{1,0:T(8,128)(2,1)} %vec.1) | copy-start | bytes 98308
  6.4 0.8 %copy-start.6 = (bf16[2,64,64]{2,1,0:T(8,128)(2,1)S(1)}, bf16[2,64,64]{2,1,0:T(8,128)(2,1)}, u32[]{:S(2)}) copy-start(bf16[2,64,64]{2,1,0:T(8,128)(2,1)} %top_b.1) | copy-start | bytes 49156
  7.2 0.7 %copy-start.7 = (s32[8,8]{1,0:T(8,128)S(1)}, s32[8,8]{1,0:T(8,128)}, u32[]{:S(2)}) copy-start(s32[8,8]{1,0:T(8,128)} %owner_v.1) | copy-start | bytes 772
  7.9 0.7 %copy-start.8 = (s32[8,8]{1,0:T(8,128)S(1)}, s32[8,8]{1,0:T(8,128)}, u32[]{:S(2)}) copy-start(s32[8,8]{1,0:T(8,128)} %member_v.1) | copy-start | bytes 772
  8.6 0.7 %copy-start.9 = (s32[32,4]{0,1:T(4,128)S(1)}, s32[32,4]{0,1:T(4,128)}, u32[]{:S(2)}) copy-start(s32[32,4]{0,1:T(4,128)} %param.15) | copy-start | bytes 1540

commit v2 on v1

--- a/solution.py
+++ b/solution.py
@@ -8,12 +8,14 @@
 from jax.sharding import PartitionSpec as P
 
 MESH = pl.DeviceIdType.MESH
+KINDS = 13
 NV = 8
 LEAF = 64
 RANK = 64
 CLUSTER_LEAVES = 4
 REACH = 4
 HALF = 64
+PLANE = 4
 WIDE = 128
 QUAD = 256
 
@@ -40,12 +42,11 @@
     far,
     root_t,
     top_b,
-    near_src,
-    owner_s,
-    count_s,
-    owner_v,
-    member_v,
-    top_src,
+    near_src_h,
+    owner_h,
+    member_h,
+    count_h,
+    top_src_h,
     out,
     vec_b,
     basis_b,
@@ -54,6 +55,12 @@
     far_b,
     root_b,
     topb_b,
+    near_src,
+    owner_s,
+    count_s,
+    owner_v,
+    member_v,
+    top_src,
     load_sem,
     pair_basis,
     ext,
@@ -61,7 +68,6 @@
     rank_b,
     rank_s,
     halo,
-    req_row,
     req,
     req_s,
     tops_row,
@@ -78,6 +84,7 @@
     smem_sem,
     send_sem,
     recv_sem,
+    known,
 ):
     o, l = lax.axis_index("owner"), lax.axis_index("local")
     me = o * locals_ + l
@@ -91,31 +98,58 @@
     left, right = lax.rem(me + total - 1, total), lax.rem(me + 1, total)
     left_id = (left // locals_, lax.rem(left, locals_))
     right_id = (right // locals_, lax.rem(right, locals_))
-    HALO, REQ, TOPS, TOPW, SKEL, PART, ROOT, FARS, SHARE, HALO2 = range(10)
+    HALO, HALO2, REST, FROM_LOW, FROM_HIGH, PASSED, TOPS, TOPW, SKEL, PART, ROOT, FARS, SHARE = range(KINDS)
+    depth = owners // PLANE
+    reach = depth // 4
+    z, y = o // PLANE, lax.rem(o, PLANE)
+    own_row = reach * PLANE
+    top_rows = 2 * reach * PLANE
+    near_rows = (2 * reach + 1) * PLANE
+    below_rows = reach * PLANE
+    above_rows = (reach - 1) * PLANE
+
+    def owner_at(dz, dy):
+        return lax.rem(z + dz + depth, depth) * PLANE + lax.rem(y + dy, PLANE)
+
+    def beside(n):
+        return owner_at(n // PLANE - reach, lax.rem(n, PLANE))
+
 
     def load(i, source, target):
         copy = pltpu.make_async_copy(source, target, load_sem.at[i])
         copy.start()
         return copy
 
-    load_vec = load(0, vec, vec_b)
-    load_basis = load(1, basis, basis_b)
-    load_up = load(2, up, up_b)
-    load_root = load(3, root_t, root_b)
-    load_topb = load(4, top_b, topb_b)
-    load_near = load(5, near, near_b)
-    load_far = load(6, far, far_b)
+    load_owner = load(0, owner_h, owner_v)
+    load_member = load(1, member_h, member_v)
+    load_vec = load(2, vec, vec_b)
+    load_basis = load(3, basis, basis_b)
+    load_up = load(4, up, up_b)
+    load_root = load(5, root_t, root_b)
+    load_top = load(6, top_src_h, top_src)
+    load_topb = load(7, top_b, topb_b)
+    load_src = load(8, near_src_h, near_src)
+    load_near = load(9, near, near_b)
+    load_owner_s = load(10, owner_h, owner_s)
+    load_count = load(11, count_h, count_s)
+    load_far = load(12, far, far_b)
 
     def remote(source, target, kind, device):
         return pltpu.make_async_remote_copy(
             src_ref=source,
             dst_ref=target,
-            send_sem=send_sem.at[kind],
+            send_sem=send_sem.at[REST if kind in (FROM_LOW, FROM_HIGH) else kind],
             recv_sem=recv_sem.at[kind],
             device_id=device,
             device_id_type=MESH,
         )
 
+    def received(ref, kind):
+        wait_bytes(ref, recv_sem.at[kind])
+
+    def sent(ref, kind):
+        wait_bytes(ref, send_sem.at[kind])
+
     barrier = pltpu.get_barrier_semaphore()
 
     def greet(device):
@@ -128,15 +162,21 @@
     greet(left_id)
     greet(right_id)
 
-    @pl.loop(1, owners)
-    def _(d):
-        greet((lax.rem(o + d, owners), l))
+    @pl.loop(0, own_row)
+    def _(n):
+        greet((beside(n), l))
+
+    @pl.loop(own_row + 1, near_rows)
+    def _(n):
+        greet((beside(n), l))
 
     lane = lax.broadcasted_iota(jnp.int32, (1, WIDE), 1)
     lanes = lax.broadcasted_iota(jnp.int32, (clusters, WIDE), 1)
     key = jnp.where(lanes >= HALF, lanes - HALF, lanes)
     named = jnp.zeros((clusters, WIDE), jnp.int32)
     member = jnp.zeros((clusters, WIDE), jnp.int32)
+    load_owner.wait()
+    load_member.wait()
     for f in range(slots):
         same = owner_v[:, f : f + 1] == key
         named = jnp.where(same, 1, named)
@@ -148,11 +188,11 @@
         rank_b[t : t + 1, :] = run
         wanted = jnp.where(run == second, wanted + member[t : t + 1], wanted)
         run = run + named[t : t + 1]
-    req_row[...] = wanted
-    req[pl.ds(o, 1), :, :] = wanted.reshape(1, 1, WIDE)
+    req[own_row] = wanted
     rank_copy = pltpu.make_async_copy(rank_b, rank_s, smem_sem.at[0])
     rank_copy.start()
     tops_row[...] = jnp.zeros((1, WIDE), jnp.int32)
+    load_top.wait()
     tops_row[:, 0:2] = top_src[...]
     tops[pl.ds(l, 1), :, :] = tops_row[...].reshape(1, 1, WIDE)
 
@@ -186,20 +226,99 @@
     load_topb.wait()
     topw[pl.ds(l, 1), :, :] = jnp.concatenate([topb_b[0], topb_b[1]], axis=1).reshape(1, RANK, WIDE)
 
-    pl.semaphore_wait(barrier, owners - 1 + locals_ - 1 + 2)
-
-    @pl.loop(1, locals_)
-    def _(d):
-        peer = (o, lax.rem(l + d, locals_))
-        own = skel.at[pl.ds(first, clusters)]
-        remote(own, own, SKEL, peer).start()
-        mine = part.at[pl.ds(l, 1)]
-        remote(mine, mine, PART, peer).start()
-
-    @pl.loop(1, owners)
-    def _(d):
-        target = req.at[pl.ds(o, 1)]
-        remote(target, target, REQ, (lax.rem(o + d, owners), l)).start()
+    pl.semaphore_wait(barrier, near_rows - 1 + locals_ - 1 + 2)
+
+    def share_skeletons():
+        @pl.loop(1, locals_)
+        def _(d):
+            peer = (o, lax.rem(l + d, locals_))
+            own = skel.at[pl.ds(first, clusters)]
+            remote(own, own, SKEL, peer).start()
+            mine = part.at[pl.ds(l, 1)]
+            remote(mine, mine, PART, peer).start()
+
+    def ask(begin, end, kind):
+        @pl.loop(begin, end)
+        def _(n):
+            row = (2 * reach - n // PLANE) * PLANE + lax.rem(PLANE - lax.rem(n, PLANE), PLANE)
+            remote(req.at[pl.ds(own_row, 1)], req.at[pl.ds(row, 1)], kind, (beside(n), l)).start()
+
+    def pass_up():
+        received(req.at[pl.ds(0, PLANE)], FROM_LOW)
+
+        @pl.loop(0, reach)
+        def _(k):
+            rows = pl.ds(near_rows + k * PLANE, PLANE)
+            remote(req.at[pl.ds(0, PLANE)], req.at[rows], PASSED, (owner_at(k + 1, 0), l)).start()
+
+    def pass_down():
+        received(req.at[pl.ds(top_rows, PLANE)], FROM_HIGH)
+
+        @pl.loop(0, reach - 1)
+        def _(k):
+            rows = pl.ds(near_rows + below_rows + k * PLANE, PLANE)
+            remote(req.at[pl.ds(top_rows, PLANE)], req.at[rows], PASSED, (owner_at(-k - 1, 0), l)).start()
+
+    away = jnp.minimum(z, depth - z)
+    late = away * 4 >= depth + 2 * reach
+    middle = (away + 1 >= reach) & (away <= reach + 1)
+    rising = z < 2 * reach
+
+    @pl.when(late)
+    def _():
+        share_skeletons()
+
+    ask(top_rows, near_rows, FROM_LOW)
+    ask(0, PLANE, FROM_HIGH)
+    for dz in (-reach, reach):
+        pl.semaphore_signal(known, inc=1, device_id=(owner_at(dz, 0), l), device_id_type=MESH)
+
+    @pl.when(jnp.logical_not(late))
+    def _():
+        share_skeletons()
+
+    ask(PLANE, own_row, REST)
+    ask(own_row + 1, top_rows, REST)
+
+    edge = REACH * LEAF
+    width = leaves * LEAF
+    remote(vec_b.at[:, pl.ds(width - edge, edge)], halo.at[0], HALO, right_id).start()
+    remote(vec_b.at[:, pl.ds(0, edge)], halo.at[1], HALO2, left_id).start()
+
+    @pl.when(middle & rising)
+    def _():
+        pass_up()
+
+    @pl.when(middle & jnp.logical_not(rising))
+    def _():
+        pass_down()
+
+    received(part.at[pl.ds(0, locals_ - 1)], PART)
+    root = part[0]
+    for other in range(1, locals_):
+        root = root + part[other]
+    root_tile[...] = root.astype(jnp.bfloat16)
+    pl.semaphore_wait(known, 2)
+
+    @pl.when(l == 0)
+    def _():
+        roots[0] = root_tile[...]
+
+    @pl.when(l != 0)
+    def _():
+        remote(root_tile, roots.at[0], ROOT, (lax.rem(o + l, owners), l)).start()
+
+    @pl.loop(1, rounds)
+    def _(i):
+        remote(root_tile, roots.at[i], ROOT, (lax.rem(o + l + locals_ * i, owners), l)).start()
+
+    @pl.when(jnp.logical_not(middle & rising))
+    def _():
+        pass_up()
+
+    @pl.when(jnp.logical_not(middle & jnp.logical_not(rising)))
+    def _():
+        pass_down()
 
     @pl.loop(1, locals_)
     def _(d):
@@ -209,61 +328,57 @@
         block = topw.at[pl.ds(l, 1)]
         remote(block, block, TOPW, peer).start()
 
-    edge = REACH * LEAF
-    width = leaves * LEAF
-    remote(vec_b.at[:, pl.ds(width - edge, edge)], halo.at[0], HALO, right_id).start()
-    remote(vec_b.at[:, pl.ds(0, edge)], halo.at[1], HALO2, left_id).start()
-
-    wait_bytes(part.at[pl.ds(0, locals_ - 1)], recv_sem.at[PART])
-    root = part[0]
-    for other in range(1, locals_):
-        root = root + part[other]
-    root_tile[...] = root.astype(jnp.bfloat16)
-
-    @pl.when(l == 0)
-    def _():
-        roots[0] = root_tile[...]
-
-    @pl.when(l != 0)
-    def _():
-        remote(root_tile, roots.at[0], ROOT, (lax.rem(o + l, owners), l)).start()
-
-    @pl.loop(1, rounds)
-    def _(i):
-        remote(root_tile, roots.at[i], ROOT, (lax.rem(o + l + locals_ * i, owners), l)).start()
-
-    wait_bytes(req.at[pl.ds(0, owners - 1)], recv_sem.at[REQ])
+    received(req.at[pl.ds(0, near_rows - 2 * PLANE - 1)], REST)
+    received(req.at[pl.ds(0, below_rows + above_rows)], PASSED)
     req_copy = pltpu.make_async_copy(req, req_s, smem_sem.at[1])
     req_copy.start()
-    wait_bytes(skel.at[pl.ds(0, clusters * (locals_ - 1))], recv_sem.at[SKEL])
+    received(skel.at[pl.ds(0, clusters * (locals_ - 1))], SKEL)
     req_copy.wait()
 
-    def chosen(asker):
-        a = skel[req_s[asker, 0, o]].astype(jnp.float32)
-        b = skel[req_s[asker, 0, HALF + o]].astype(jnp.float32)
+    def chosen(n):
+        a = skel[req_s[n, 0, o]].astype(jnp.float32)
+        b = skel[req_s[n, 0, HALF + o]].astype(jnp.float32)
         return jnp.where(low, a, b).astype(jnp.bfloat16).reshape(1, NV, WIDE)
 
-    far_recv[pl.ds(o, 1), :, :] = chosen(o)
-
-    @pl.loop(1, owners)
-    def _(d):
-        asker = lax.rem(o + d, owners)
-        far_send[pl.ds(asker, 1), :, :] = chosen(asker)
-        remote(far_send.at[pl.ds(asker, 1)], far_recv.at[pl.ds(o, 1)], FARS, (asker, l)).start()
-
-    wait_bytes(tops.at[pl.ds(0, locals_ - 1)], recv_sem.at[TOPS])
+    def answer(n, asker):
+        far_send[pl.ds(n, 1), :, :] = chosen(n)
+        remote(far_send.at[pl.ds(n, 1)], far_recv.at[pl.ds(o, 1)], FARS, (asker, l)).start()
+
+    @pl.loop(0, below_rows)
+    def _(i):
+        j = below_rows - 1 - i
+        answer(near_rows + j, owner_at(-reach - 1 - j // PLANE, lax.rem(j, PLANE)))
+
+    if above_rows:
+
+        @pl.loop(0, above_rows)
+        def _(i):
+            j = above_rows - 1 - i
+            answer(near_rows + below_rows + j, owner_at(reach + 1 + j // PLANE, lax.rem(j, PLANE)))
+
+    @pl.loop(0, own_row)
+    def _(n):
+        answer(n, beside(n))
+
+    @pl.loop(own_row + 1, near_rows)
+    def _(n):
+        answer(n, beside(n))
+
+    far_recv[pl.ds(o, 1), :, :] = chosen(own_row)
+
+    received(tops.at[pl.ds(0, locals_ - 1)], TOPS)
     tops_copy = pltpu.make_async_copy(tops, tops_s, smem_sem.at[2])
     tops_copy.start()
-    wait_bytes(topw.at[pl.ds(0, locals_ - 1)], recv_sem.at[TOPW])
+    received(topw.at[pl.ds(0, locals_ - 1)], TOPW)
     tops_copy.wait()
 
     @pl.when(l == 0)
     def _():
-        wait_bytes(roots.at[pl.ds(0, rounds - 1)], recv_sem.at[ROOT])
+        received(roots.at[pl.ds(0, rounds - 1)], ROOT)
 
     @pl.when(l != 0)
     def _():
-        wait_bytes(roots, recv_sem.at[ROOT])
+        received(roots, ROOT)
 
     def coupled(s):
         away = lax.rem(o - l - tops_s[s // 2, 0, s % 2] + 2 * owners, owners)
@@ -282,8 +397,8 @@
         mine = share.at[pl.ds(l, 1)]
         remote(mine, mine, SHARE, (o, lax.rem(l + d, locals_))).start()
 
-    wait_bytes(halo.at[0], recv_sem.at[HALO])
-    wait_bytes(halo.at[1], recv_sem.at[HALO2])
+    received(halo.at[0], HALO)
+    received(halo.at[1], HALO2)
 
     def spread(pair, at):
         pair = pair.astype(jnp.float32)
@@ -296,6 +411,7 @@
         spread(halo[1, :, q * WIDE : (q + 1) * WIDE], REACH + leaves + 2 * q)
     for q in range(pairs):
         spread(vec_b[:, q * WIDE : (q + 1) * WIDE], REACH + 2 * q)
+    load_src.wait()
     load_near.wait()
     zero = jnp.zeros((NV, WIDE), jnp.float32)
 
@@ -323,16 +439,18 @@
                 [acc[c * NV : (c + 1) * NV], acc[(c + 1) * NV : (c + 2) * NV]], axis=1
             )
 
-    wait_bytes(share.at[pl.ds(0, locals_ - 1)], recv_sem.at[SHARE])
+    received(share.at[pl.ds(0, locals_ - 1)], SHARE)
     summed = share[0]
     for other in range(1, locals_):
         summed = summed + share[other]
     root_out = summed[:, 0:RANK].astype(jnp.bfloat16)
     downward = dot(root_out, root_b[...])
     rank_copy.wait()
+    load_owner_s.wait()
+    load_count.wait()
     load_far.wait()
 
-    wait_bytes(far_recv.at[pl.ds(0, owners - 1)], recv_sem.at[FARS])
+    received(far_recv.at[pl.ds(0, owners - 1)], FARS)
 
     def picked(t, f):
         source = owner_s[t, f]
@@ -354,24 +472,25 @@
                 result = dot(leaf_out[:, c * WIDE : (c + 1) * WIDE], pair_basis[q]) + near_res[q]
                 out[:, q * WIDE : (q + 1) * WIDE] = result.astype(jnp.bfloat16)
 
-    wait_bytes(skel.at[pl.ds(0, clusters * (locals_ - 1))], send_sem.at[SKEL])
-    wait_bytes(part.at[pl.ds(0, locals_ - 1)], send_sem.at[PART])
-    wait_bytes(req.at[pl.ds(0, owners - 1)], send_sem.at[REQ])
-    wait_bytes(tops.at[pl.ds(0, locals_ - 1)], send_sem.at[TOPS])
-    wait_bytes(topw.at[pl.ds(0, locals_ - 1)], send_sem.at[TOPW])
-    wait_bytes(halo.at[0], send_sem.at[HALO])
-    wait_bytes(halo.at[1], send_sem.at[HALO2])
+    sent(skel.at[pl.ds(0, clusters * (locals_ - 1))], SKEL)
+    sent(part.at[pl.ds(0, locals_ - 1)], PART)
+    sent(req.at[pl.ds(0, near_rows - 1)], REST)
+    sent(req.at[pl.ds(0, below_rows + above_rows)], PASSED)
+    sent(tops.at[pl.ds(0, locals_ - 1)], TOPS)
+    sent(topw.at[pl.ds(0, locals_ - 1)], TOPW)
+    sent(halo.at[0], HALO)
+    sent(halo.at[1], HALO2)
 
     @pl.when(l == 0)
     def _():
-        wait_bytes(roots.at[pl.ds(0, rounds - 1)], send_sem.at[ROOT])
+        sent(roots.at[pl.ds(0, rounds - 1)], ROOT)
 
     @pl.when(l != 0)
     def _():
-        wait_bytes(roots, send_sem.at[ROOT])
-
-    wait_bytes(share.at[pl.ds(0, locals_ - 1)], send_sem.at[SHARE])
-    wait_bytes(far_recv.at[pl.ds(0, owners - 1)], send_sem.at[FARS])
+        sent(roots, ROOT)
+
+    sent(share.at[pl.ds(0, locals_ - 1)], SHARE)
+    sent(far_recv.at[pl.ds(0, owners - 1)], FARS)
 
 
 def per_device(
@@ -393,25 +512,29 @@
     clusters = far_owner.shape[0]
     leaves = clusters * CLUSTER_LEAVES
     bf16, f32, i32 = jnp.bfloat16, jnp.float32, jnp.int32
-    hbm = pl.BlockSpec(memory_space=pl.ANY)
-    smem = pl.BlockSpec(memory_space=pltpu.SMEM)
+    hbm = pl.BlockSpec(memory_space=pltpu.HBM)
     vmem = pl.BlockSpec(memory_space=pltpu.VMEM)
     big = (vectors, leaf_basis, near_blocks, up_transfer, far_blocks, root_transfer, top_blocks)
     return pl.pallas_call(
         functools.partial(kernel, owners, locals_),
         out_shape=jax.ShapeDtypeStruct(vectors.shape, bf16),
-        in_specs=[hbm] * 7 + [smem] * 3 + [vmem] * 3,
+        in_specs=[hbm] * 12,
         out_specs=vmem,
         scratch_shapes=[pltpu.VMEM(a.shape, bf16) for a in big]
         + [
-            pltpu.SemaphoreType.DMA((7,)),
+            pltpu.SMEM((near_source.shape[1], near_source.shape[0]), i32),
+            pltpu.SMEM(far_owner.shape, i32),
+            pltpu.SMEM(far_count.shape, i32),
+            pltpu.VMEM(far_owner.shape, i32),
+            pltpu.VMEM(far_owner.shape, i32),
+            pltpu.VMEM(top_source.shape, i32),
+            pltpu.SemaphoreType.DMA((13,)),
             pltpu.VMEM((leaves // 2, WIDE, WIDE), bf16),
             pltpu.VMEM((leaves + 2 * REACH, NV, WIDE), f32),
             pltpu.VMEM((leaves // 2, NV, WIDE), f32),
             pltpu.VMEM((clusters, WIDE), i32),
             pltpu.SMEM((clusters, WIDE), i32),
             pltpu.VMEM((2, NV, REACH * LEAF), bf16),
-            pltpu.VMEM((1, WIDE), i32),
             pltpu.VMEM((owners, 1, WIDE), i32),
             pltpu.SMEM((owners, 1, WIDE), i32),
             pltpu.VMEM((1, WIDE), i32),
@@ -426,13 +549,14 @@
             pltpu.VMEM((owners, NV, WIDE), bf16),
             pltpu.VMEM((locals_, NV, WIDE), f32),
             pltpu.SemaphoreType.DMA((3,)),
-            pltpu.SemaphoreType.DMA((10,)),
-            pltpu.SemaphoreType.DMA((10,)),
+            pltpu.SemaphoreType.DMA((KINDS,)),
+            pltpu.SemaphoreType.DMA((KINDS,)),
+            pltpu.SemaphoreType.REGULAR,
         ],
         compiler_params=pltpu.CompilerParams(
-            collective_id=0, has_side_effects=True, vmem_limit_bytes=32 * 1024 * 1024
+            collective_id=0, has_side_effects=True, vmem_limit_bytes=63 * 1024 * 1024
         ),
-    )(*big, near_source.T, far_owner, far_count, far_owner, far_member, top_source)
+    )(*big, near_source.T, far_owner, far_member, far_count, top_source)
 
 
 def solution(mesh):

time: 52.3 us -> 39.3 us (0.75)
  the two profiles are of different devices: /device:TPU:4 before, /device:TPU:2 now
where the time goes in v2:
time: 39.3 us; the launch traced here: 39.1 us
  Pallas kernels  37.7 us (96%)
  local copies, waits for them, and re-layouts  1.38 us (4%)
    pallas_call x1, Pallas kernels, per_device(): pl.pallas_call(functools.partial(kernel, owners, locals_), out_shape=jax....  37.7 us
    unnamed x1, local copies, waits for them, and re-layouts  1.38 us

profile of v2, /device:TPU:2, one launch (start us, length us, event | category | flops | bytes accessed | tf_op | source)
XLA Modules:
  0.0 39.1 jit_solution(18012041878530224902)
XLA Ops:
  0.0 37.7 %shard_map.118 = bf16[8,2048]{1,0:T(8,128)(2,1)} custom-call(bf16[8,2048]{1,0:T(8,128)(2,1)} %vec.1, bf16[64,2048]{1,0:T(8,128)(2,1)} %basis.1, bf16[4,64,2048]{2,1,0:T(8,128)(2,1)} %near.1, bf16[64,2048]{1,0:T(8,128)(2,1)} %up.1, bf16[8,64,512]{2,1,0:T(8,128)(2,1)} %far.1, bf16[64,512]{1,0:T(8,128)(2,1)} %root_t.1, bf16[2,64,64]{2,1,0:T(8,128)(2,1)} %top_b.1, ...), custom_call_target="tpu_custom_call" | custom-call | tf_op jit(solution)/shard_map/pallas_call | solution.py:518
  37.7 1.4 %copy.14 = bf16[8,2048]{1,0:T(8,128)(2,1)} copy(bf16[8,2048]{1,0:T(8,128)(2,1)} %shard_map.118) | data formatting | bytes 65536

commit v3 on v2

--- a/solution.py
+++ b/solution.py
@@ -115,6 +115,44 @@
         return owner_at(n // PLANE - reach, lax.rem(n, PLANE))
 
 
+    def remote(source, target, kind, device):
+        return pltpu.make_async_remote_copy(
+            src_ref=source,
+            dst_ref=target,
+            send_sem=send_sem.at[REST if kind in (FROM_LOW, FROM_HIGH) else kind],
+            recv_sem=recv_sem.at[kind],
+            device_id=device,
+            device_id_type=MESH,
+        )
+
+    def received(ref, kind):
+        wait_bytes(ref, recv_sem.at[kind])
+
+    def sent(ref, kind):
+        wait_bytes(ref, send_sem.at[kind])
+
+    barrier = pltpu.get_barrier_semaphore()
+
+    def greet(device):
+        pl.semaphore_signal(barrier, inc=1, device_id=device, device_id_type=MESH)
+
+    def greet_planes(begin, end):
+        @pl.loop(begin, end, unroll=True)
+        def _(n):
+            greet((beside(n), l))
+
+    greet_planes(0, PLANE)
+    greet_planes(top_rows, near_rows)
+    greet_planes(PLANE, own_row)
+    greet_planes(own_row + 1, top_rows)
+
+    @pl.loop(1, locals_, unroll=True)
+    def _(d):
+        greet((o, lax.rem(l + d, locals_)))
+
+    greet(left_id)
+    greet(right_id)
+
     def load(i, source, target):
         copy = pltpu.make_async_copy(source, target, load_sem.at[i])
         copy.start()
@@ -133,42 +171,6 @@
     load_owner_s = load(10, owner_h, owner_s)
     load_count = load(11, count_h, count_s)
     load_far = load(12, far, far_b)
-
-    def remote(source, target, kind, device):
-        return pltpu.make_async_remote_copy(
-            src_ref=source,
-            dst_ref=target,
-            send_sem=send_sem.at[REST if kind in (FROM_LOW, FROM_HIGH) else kind],
-            recv_sem=recv_sem.at[kind],
-            device_id=device,
-            device_id_type=MESH,
-        )
-
-    def received(ref, kind):
-        wait_bytes(ref, recv_sem.at[kind])
-
-    def sent(ref, kind):
-        wait_bytes(ref, send_sem.at[kind])
-
-    barrier = pltpu.get_barrier_semaphore()
-
-    def greet(device):
-        pl.semaphore_signal(barrier, inc=1, device_id=device, device_id_type=MESH)
-
-    @pl.loop(1, locals_)
-    def _(d):
-        greet((o, lax.rem(l + d, locals_)))
-
-    greet(left_id)
-    greet(right_id)
-
-    @pl.loop(0, own_row)
-    def _(n):
-        greet((beside(n), l))
-
-    @pl.loop(own_row + 1, near_rows)
-    def _(n):
-        greet((beside(n), l))
 
     lane = lax.broadcasted_iota(jnp.int32, (1, WIDE), 1)
     lanes = lax.broadcasted_iota(jnp.int32, (clusters, WIDE), 1)
@@ -229,24 +231,26 @@
     pl.semaphore_wait(barrier, near_rows - 1 + locals_ - 1 + 2)
 
     def share_skeletons():
-        @pl.loop(1, locals_)
+        @pl.loop(1, locals_, unroll=True)
         def _(d):
-            peer = (o, lax.rem(l + d, locals_))
+            mine = part.at[pl.ds(l, 1)]
+            remote(mine, mine, PART, (o, lax.rem(l + d, locals_))).start()
+
+        @pl.loop(1, locals_, unroll=True)
+        def _(d):
             own = skel.at[pl.ds(first, clusters)]
-            remote(own, own, SKEL, peer).start()
-            mine = part.at[pl.ds(l, 1)]
-            remote(mine, mine, PART, peer).start()
+            remote(own, own, SKEL, (o, lax.rem(l + d, locals_))).start()
 
     def ask(begin, end, kind):
-        @pl.loop(begin, end)
+        @pl.loop(begin, end, unroll=True)
         def _(n):
             row = (2 * reach - n // PLANE) * PLANE + lax.rem(PLANE - lax.rem(n, PLANE), PLANE)
-            remote(req.at[pl.ds(own_row, 1)], req.at[pl.ds(row, 1)], kind, (beside(n), l)).start()
+            remote(req.at[own_row], req.at[row], kind, (beside(n), l)).start()
 
     def pass_up():
         received(req.at[pl.ds(0, PLANE)], FROM_LOW)
 
-        @pl.loop(0, reach)
+        @pl.loop(0, reach, unroll=True)
         def _(k):
             rows = pl.ds(near_rows + k * PLANE, PLANE)
             remote(req.at[pl.ds(0, PLANE)], req.at[rows], PASSED, (owner_at(k + 1, 0), l)).start()
@@ -254,7 +258,7 @@
     def pass_down():
         received(req.at[pl.ds(top_rows, PLANE)], FROM_HIGH)
 
-        @pl.loop(0, reach - 1)
+        @pl.loop(0, reach - 1, unroll=True)
         def _(k):
             rows = pl.ds(near_rows + below_rows + k * PLANE, PLANE)
             remote(req.at[pl.ds(top_rows, PLANE)], req.at[rows], PASSED, (owner_at(-k - 1, 0), l)).start()
@@ -308,7 +312,7 @@
     def _():
         remote(root_tile, roots.at[0], ROOT, (lax.rem(o + l, owners), l)).start()
 
-    @pl.loop(1, rounds)
+    @pl.loop(1, rounds, unroll=True)
     def _(i):
         remote(root_tile, roots.at[i], ROOT, (lax.rem(o + l + locals_ * i, owners), l)).start()
 
@@ -320,7 +324,7 @@
     def _():
         pass_down()
 
-    @pl.loop(1, locals_)
+    @pl.loop(1, locals_, unroll=True)
     def _(d):
         peer = (o, lax.rem(l + d, locals_))
         mine = tops.at[pl.ds(l, 1)]
@@ -328,12 +332,15 @@
         block = topw.at[pl.ds(l, 1)]
         remote(block, block, TOPW, peer).start()
 
+    def to_scalars(rows, sem):
+        copy = pltpu.make_async_copy(req.at[rows], req_s.at[rows], sem)
+        copy.start()
+        return copy
+
     received(req.at[pl.ds(0, near_rows - 2 * PLANE - 1)], REST)
-    received(req.at[pl.ds(0, below_rows + above_rows)], PASSED)
-    req_copy = pltpu.make_async_copy(req, req_s, smem_sem.at[1])
-    req_copy.start()
+    near_asked = to_scalars(pl.ds(0, near_rows), smem_sem.at[1])
     received(skel.at[pl.ds(0, clusters * (locals_ - 1))], SKEL)
-    req_copy.wait()
+    near_asked.wait()
 
     def chosen(n):
         a = skel[req_s[n, 0, o]].astype(jnp.float32)
@@ -344,25 +351,29 @@
         far_send[pl.ds(n, 1), :, :] = chosen(n)
         remote(far_send.at[pl.ds(n, 1)], far_recv.at[pl.ds(o, 1)], FARS, (asker, l)).start()
 
-    @pl.loop(0, below_rows)
+    @pl.loop(0, own_row, unroll=True)
+    def _(n):
+        answer(n, beside(n))
+
+    @pl.loop(own_row + 1, near_rows, unroll=True)
+    def _(n):
+        answer(n, beside(n))
+
+    received(req.at[pl.ds(0, below_rows + above_rows)], PASSED)
+    far_asked = to_scalars(pl.ds(near_rows, below_rows + above_rows), smem_sem.at[3])
+    far_asked.wait()
+
+    @pl.loop(0, below_rows, unroll=True)
     def _(i):
         j = below_rows - 1 - i
         answer(near_rows + j, owner_at(-reach - 1 - j // PLANE, lax.rem(j, PLANE)))
 
     if above_rows:
 
-        @pl.loop(0, above_rows)
+        @pl.loop(0, above_rows, unroll=True)
         def _(i):
             j = above_rows - 1 - i
             answer(near_rows + below_rows + j, owner_at(reach + 1 + j // PLANE, lax.rem(j, PLANE)))
-
-    @pl.loop(0, own_row)
-    def _(n):
-        answer(n, beside(n))
-
-    @pl.loop(own_row + 1, near_rows)
-    def _(n):
-        answer(n, beside(n))
 
     far_recv[pl.ds(o, 1), :, :] = chosen(own_row)
 
@@ -392,7 +403,7 @@
         total_share = total_share + dot_t(lhs, jnp.concatenate([block, block], axis=0))
     share[pl.ds(l, 1), :, :] = total_share.reshape(1, NV, WIDE)
 
-    @pl.loop(1, locals_)
+    @pl.loop(1, locals_, unroll=True)
     def _(d):
         mine = share.at[pl.ds(l, 1)]
         remote(mine, mine, SHARE, (o, lax.rem(l + d, locals_))).start()
@@ -548,7 +559,7 @@
             pltpu.VMEM((owners, NV, WIDE), bf16),
             pltpu.VMEM((owners, NV, WIDE), bf16),
             pltpu.VMEM((locals_, NV, WIDE), f32),
-            pltpu.SemaphoreType.DMA((3,)),
+            pltpu.SemaphoreType.DMA((4,)),
             pltpu.SemaphoreType.DMA((KINDS,)),
             pltpu.SemaphoreType.DMA((KINDS,)),
             pltpu.SemaphoreType.REGULAR,

time: 39.3 us -> 38.1 us (0.969)
  the two profiles are of different devices: /device:TPU:2 before, /device:TPU:4 now
where the time goes in v3:
time: 38.1 us; the launch traced here: 37.9 us
  Pallas kernels  36.6 us (96%)
  local copies, waits for them, and re-layouts  1.38 us (4%)
    pallas_call x1, Pallas kernels, per_device(): pl.pallas_call(functools.partial(kernel, owners, locals_), out_shape=jax....  36.6 us
    unnamed x1, local copies, waits for them, and re-layouts  1.38 us

profile of v3, /device:TPU:4, one launch (start us, length us, event | category | flops | bytes accessed | tf_op | source)
XLA Modules:
  0.0 37.9 jit_solution(8516522993423740439)
XLA Ops:
  0.0 36.6 %shard_map.118 = bf16[8,2048]{1,0:T(8,128)(2,1)} custom-call(bf16[8,2048]{1,0:T(8,128)(2,1)} %vec.1, bf16[64,2048]{1,0:T(8,128)(2,1)} %basis.1, bf16[4,64,2048]{2,1,0:T(8,128)(2,1)} %near.1, bf16[64,2048]{1,0:T(8,128)(2,1)} %up.1, bf16[8,64,512]{2,1,0:T(8,128)(2,1)} %far.1, bf16[64,512]{1,0:T(8,128)(2,1)} %root_t.1, bf16[2,64,64]{2,1,0:T(8,128)(2,1)} %top_b.1, ...), custom_call_target="tpu_custom_call" | custom-call | tf_op jit(solution)/shard_map/pallas_call | solution.py:529
  36.6 1.4 %copy.14 = bf16[8,2048]{1,0:T(8,128)(2,1)} copy(bf16[8,2048]{1,0:T(8,128)(2,1)} %shard_map.118) | data formatting | bytes 65536

commit v4 on v3

--- a/solution.py
+++ b/solution.py
@@ -75,6 +75,7 @@
     tops_s,
     topw,
     skel,
+    skel_rows,
     part,
     root_tile,
     roots,
@@ -205,19 +206,23 @@
     load_basis.wait()
     load_up.wait()
     first = l * clusters
-    tiles = []
-    for t in range(clusters):
+
+    @pl.loop(0, clusters)
+    def _(t):
         parts = []
-        for q in (2 * t, 2 * t + 1):
-            block = basis_b[:, q * WIDE : (q + 1) * WIDE]
+        for c in range(2):
+            q = 2 * t + c
+            lanes_q = pl.ds(pl.multiple_of(q * WIDE, WIDE), WIDE)
+            block = basis_b[:, lanes_q]
             diagonal = jnp.concatenate([block * low_ones, block * high_ones], axis=0)
             pair_basis[q] = diagonal
-            parts.append(dot_t(vec_b[:, q * WIDE : (q + 1) * WIDE], diagonal))
+            parts.append(dot_t(vec_b[:, lanes_q], diagonal))
         leaf_skel = jnp.concatenate(parts, axis=1).astype(jnp.bfloat16)
-        block = up_b[:, t * QUAD : (t + 1) * QUAD]
+        block = up_b[:, pl.ds(pl.multiple_of(t * QUAD, QUAD), QUAD)]
         tile = dot_t(leaf_skel, jnp.concatenate([block, block], axis=0)).astype(jnp.bfloat16)
         skel[pl.ds(first + t, 1), :, :] = tile.reshape(1, NV, WIDE)
-        tiles.append(tile.astype(jnp.float32))
+
+    tiles = [skel[first + t].astype(jnp.float32) for t in range(clusters)]
     load_root.wait()
     rows = jnp.concatenate(
         [jnp.where(low, tiles[2 * q], tiles[2 * q + 1]) for q in range(clusters // 2)], axis=1
@@ -347,9 +352,15 @@
         b = skel[req_s[n, 0, HALF + o]].astype(jnp.float32)
         return jnp.where(low, a, b).astype(jnp.bfloat16).reshape(1, NV, WIDE)
 
+    def choose(begin, end):
+        @pl.loop(begin, end, unroll=True)
+        def _(n):
+            far_send[pl.ds(n, 1), :, :] = chosen(n)
+
     def answer(n, asker):
-        far_send[pl.ds(n, 1), :, :] = chosen(n)
         remote(far_send.at[pl.ds(n, 1)], far_recv.at[pl.ds(o, 1)], FARS, (asker, l)).start()
+
+    choose(0, near_rows)
 
     @pl.loop(0, own_row, unroll=True)
     def _(n):
@@ -359,23 +370,54 @@
     def _(n):
         answer(n, beside(n))
 
+    members = clusters * locals_
+    skel_rows[...] = skel[...].astype(jnp.float32).reshape(members * NV, WIDE).astype(jnp.bfloat16)
+    column = lax.broadcasted_iota(jnp.int32, (1, NV, members * NV), 2)
+    row = lax.broadcasted_iota(jnp.int32, (1, NV, members * NV), 1)
+    member_of = jnp.where(lax.rem(column, NV) == row, column // NV, -1).astype(jnp.float32)
     received(req.at[pl.ds(0, below_rows + above_rows)], PASSED)
-    far_asked = to_scalars(pl.ds(near_rows, below_rows + above_rows), smem_sem.at[3])
-    far_asked.wait()
-
-    @pl.loop(0, below_rows, unroll=True)
-    def _(i):
-        j = below_rows - 1 - i
-        answer(near_rows + j, owner_at(-reach - 1 - j // PLANE, lax.rem(j, PLANE)))
-
-    if above_rows:
-
+    passed = req[near_rows:owners].astype(jnp.float32)
+    at = lax.broadcasted_iota(jnp.int32, passed.shape, 2)
+    ones = [
+        (jnp.sum(jnp.where(at == o + half, passed, 0.0), axis=2, keepdims=True) == member_of).astype(jnp.float32)
+        for half in (0, HALF)
+    ]
+    rows = (owners - near_rows) * NV
+    both = jnp.concatenate([one.reshape(rows, members * NV) for one in ones], axis=0).astype(jnp.bfloat16)
+    both = dot(both, skel_rows[...])
+    wide_low = lax.broadcasted_iota(jnp.int32, (rows, WIDE), 1) < HALF
+    both = jnp.where(wide_low, both[:rows], both[rows:])
+    far_send[near_rows:owners] = both.reshape(owners - near_rows, NV, WIDE).astype(jnp.bfloat16)
+
+    def answer_below():
+        @pl.loop(0, below_rows, unroll=True)
+        def _(i):
+            j = below_rows - 1 - i
+            answer(near_rows + j, owner_at(-reach - 1 - j // PLANE, lax.rem(j, PLANE)))
+
+    def answer_above():
         @pl.loop(0, above_rows, unroll=True)
         def _(i):
             j = above_rows - 1 - i
             answer(near_rows + below_rows + j, owner_at(reach + 1 + j // PLANE, lax.rem(j, PLANE)))
 
-    far_recv[pl.ds(o, 1), :, :] = chosen(own_row)
+    above_first = (z > 2 * reach) & (z < 3 * reach)
+
+    if above_rows:
+
+        @pl.when(above_first)
+        def _():
+            answer_above()
+
+    answer_below()
+
+    if above_rows:
+
+        @pl.when(jnp.logical_not(above_first))
+        def _():
+            answer_above()
+
+    far_recv[pl.ds(o, 1), :, :] = far_send[pl.ds(own_row, 1), :, :]
 
     received(tops.at[pl.ds(0, locals_ - 1)], TOPS)
     tops_copy = pltpu.make_async_copy(tops, tops_s, smem_sem.at[2])
@@ -420,8 +462,10 @@
     for q in range(REACH // 2):
         spread(halo[0, :, q * WIDE : (q + 1) * WIDE], 2 * q)
         spread(halo[1, :, q * WIDE : (q + 1) * WIDE], REACH + leaves + 2 * q)
-    for q in range(pairs):
-        spread(vec_b[:, q * WIDE : (q + 1) * WIDE], REACH + 2 * q)
+    @pl.loop(0, pairs, unroll=4)
+    def _(q):
+        spread(vec_b[:, pl.ds(pl.multiple_of(q * WIDE, WIDE), WIDE)], REACH + 2 * q)
+
     load_src.wait()
     load_near.wait()
     zero = jnp.zeros((NV, WIDE), jnp.float32)
@@ -440,11 +484,12 @@
     def inside(at):
         return jnp.minimum(jnp.maximum(at, 0), leaves + 2 * REACH - 1)
 
-    for t in range(clusters):
+    @pl.loop(0, clusters)
+    def _(t):
         acc = jnp.zeros((CLUSTER_LEAVES * NV, LEAF), jnp.float32)
         for i in range(near_slots):
             lhs = quad([ext[inside(near_src[i, CLUSTER_LEAVES * t + c] + offset)] for c in range(CLUSTER_LEAVES)])
-            acc = acc + dot_t(lhs, near_b[i, :, t * QUAD : (t + 1) * QUAD])
+            acc = acc + dot_t(lhs, near_b[i, :, pl.ds(pl.multiple_of(t * QUAD, QUAD), QUAD)])
         for c in range(0, CLUSTER_LEAVES, 2):
             near_res[2 * t + c // 2] = jnp.concatenate(
                 [acc[c * NV : (c + 1) * NV], acc[(c + 1) * NV : (c + 2) * NV]], axis=1
@@ -528,7 +573,7 @@
     big = (vectors, leaf_basis, near_blocks, up_transfer, far_blocks, root_transfer, top_blocks)
     return pl.pallas_call(
         functools.partial(kernel, owners, locals_),
-        out_shape=jax.ShapeDtypeStruct(vectors.shape, bf16),
+        out_shape=pltpu.VMEM(vectors.shape, bf16),
         in_specs=[hbm] * 12,
         out_specs=vmem,
         scratch_shapes=[pltpu.VMEM(a.shape, bf16) for a in big]
@@ -553,21 +598,22 @@
             pltpu.SMEM((locals_, 1, WIDE), i32),
             pltpu.VMEM((locals_, RANK, WIDE), bf16),
             pltpu.VMEM((clusters * locals_, NV, WIDE), bf16),
+            pltpu.VMEM((clusters * locals_ * NV, WIDE), bf16),
             pltpu.VMEM((locals_, NV, WIDE), f32),
             pltpu.VMEM((NV, WIDE), bf16),
             pltpu.VMEM((owners // locals_, NV, WIDE), bf16),
             pltpu.VMEM((owners, NV, WIDE), bf16),
             pltpu.VMEM((owners, NV, WIDE), bf16),
             pltpu.VMEM((locals_, NV, WIDE), f32),
-            pltpu.SemaphoreType.DMA((4,)),
+            pltpu.SemaphoreType.DMA((3,)),
             pltpu.SemaphoreType.DMA((KINDS,)),
             pltpu.SemaphoreType.DMA((KINDS,)),
             pltpu.SemaphoreType.REGULAR,
         ],
         compiler_params=pltpu.CompilerParams(
-            collective_id=0, has_side_effects=True, vmem_limit_bytes=63 * 1024 * 1024
+            collective_id=0, has_side_effects=True, vmem_limit_bytes=32 * 1024 * 1024
         ),
-    )(*big, near_source.T, far_owner, far_member, far_count, top_source)
+    )(*[pltpu.with_memory_space_constraint(a, pltpu.HBM) for a in (*big, near_source.T, far_owner, far_member, far_count, top_source)])
 
 
 def solution(mesh):

time: 38.1 us -> 35.9 us (0.942)
  the two profiles are of different devices: /device:TPU:4 before, /device:TPU:2 now
where the time goes in v4:
time: 35.9 us; the launch traced here: 35.7 us
  Pallas kernels  35.1 us (98%)
  local copies, waits for them, and re-layouts  0.62 us (2%)
    pallas_call x1, Pallas kernels, per_device(): pl.pallas_call(functools.partial(kernel, owners, locals_), out_shape=pltp...  35.1 us

profile of v4, /device:TPU:2, one launch (start us, length us, event | category | flops | bytes accessed | tf_op | source)
XLA Modules:
  0.0 35.7 jit_solution(17160820446338822290)
XLA Ops:
  0.0 35.1 %shard_map.118 = bf16[8,2048]{1,0:T(8,128)(2,1)S(1)} custom-call(bf16[8,2048]{1,0:T(8,128)(2,1)} %vec.1, bf16[64,2048]{1,0:T(8,128)(2,1)} %basis.1, bf16[4,64,2048]{2,1,0:T(8,128)(2,1)} %near.1, bf16[64,2048]{1,0:T(8,128)(2,1)} %up.1, bf16[8,64,512]{2,1,0:T(8,128)(2,1)} %far.1, bf16[64,512]{1,0:T(8,128)(2,1)} %root_t.1, bf16[2,64,64]{2,1,0:T(8,128)(2,1)} %top_b.1, ...), custom_call_target="tpu_custom_call" | custom-call | tf_op jit(solution)/shard_map/pallas_call | solution.py:574
  35.1 0.6 %copy.14 = bf16[8,2048]{1,0:T(8,128)(2,1)} copy(bf16[8,2048]{1,0:T(8,128)(2,1)S(1)} %shard_map.118) | data formatting | bytes 65536

commit v5 on v4

--- a/solution.py
+++ b/solution.py
@@ -8,7 +8,7 @@
 from jax.sharding import PartitionSpec as P
 
 MESH = pl.DeviceIdType.MESH
-KINDS = 13
+KINDS = 14
 NV = 8
 LEAF = 64
 RANK = 64
@@ -99,7 +99,7 @@
     left, right = lax.rem(me + total - 1, total), lax.rem(me + 1, total)
     left_id = (left // locals_, lax.rem(left, locals_))
     right_id = (right // locals_, lax.rem(right, locals_))
-    HALO, HALO2, REST, FROM_LOW, FROM_HIGH, PASSED, TOPS, TOPW, SKEL, PART, ROOT, FARS, SHARE = range(KINDS)
+    HALO, HALO2, REST, FROM_LOW, FROM_HIGH, PASSED, TOPS, TOPW, SKEL, PART, ROOT, FARS, SHARE, PASSED_DOWN = range(KINDS)
     depth = owners // PLANE
     reach = depth // 4
     z, y = o // PLANE, lax.rem(o, PLANE)
@@ -132,6 +132,15 @@
     def sent(ref, kind):
         wait_bytes(ref, send_sem.at[kind])
 
+    def load(i, source, target):
+        copy = pltpu.make_async_copy(source, target, load_sem.at[i])
+        copy.start()
+        return copy
+
+    load_vec = load(2, vec, vec_b)
+    load_basis = load(3, basis, basis_b)
+    load_up = load(4, up, up_b)
+
     barrier = pltpu.get_barrier_semaphore()
 
     def greet(device):
@@ -154,16 +163,8 @@
     greet(left_id)
     greet(right_id)
 
-    def load(i, source, target):
-        copy = pltpu.make_async_copy(source, target, load_sem.at[i])
-        copy.start()
-        return copy
-
     load_owner = load(0, owner_h, owner_v)
     load_member = load(1, member_h, member_v)
-    load_vec = load(2, vec, vec_b)
-    load_basis = load(3, basis, basis_b)
-    load_up = load(4, up, up_b)
     load_root = load(5, root_t, root_b)
     load_top = load(6, top_src_h, top_src)
     load_topb = load(7, top_b, topb_b)
@@ -266,7 +267,7 @@
         @pl.loop(0, reach - 1, unroll=True)
         def _(k):
             rows = pl.ds(near_rows + below_rows + k * PLANE, PLANE)
-            remote(req.at[pl.ds(top_rows, PLANE)], req.at[rows], PASSED, (owner_at(-k - 1, 0), l)).start()
+            remote(req.at[pl.ds(top_rows, PLANE)], req.at[rows], PASSED_DOWN, (owner_at(-k - 1, 0), l)).start()
 
     away = jnp.minimum(z, depth - z)
     late = away * 4 >= depth + 2 * reach
@@ -288,46 +289,6 @@
 
     ask(PLANE, own_row, REST)
     ask(own_row + 1, top_rows, REST)
-
-    edge = REACH * LEAF
-    width = leaves * LEAF
-    remote(vec_b.at[:, pl.ds(width - edge, edge)], halo.at[0], HALO, right_id).start()
-    remote(vec_b.at[:, pl.ds(0, edge)], halo.at[1], HALO2, left_id).start()
-
-    @pl.when(middle & rising)
-    def _():
-        pass_up()
-
-    @pl.when(middle & jnp.logical_not(rising))
-    def _():
-        pass_down()
-
-    received(part.at[pl.ds(0, locals_ - 1)], PART)
-    root = part[0]
-    for other in range(1, locals_):
-        root = root + part[other]
-    root_tile[...] = root.astype(jnp.bfloat16)
-    pl.semaphore_wait(known, 2)
-
-    @pl.when(l == 0)
-    def _():
-        roots[0] = root_tile[...]
-
-    @pl.when(l != 0)
-    def _():
-        remote(root_tile, roots.at[0], ROOT, (lax.rem(o + l, owners), l)).start()
-
-    @pl.loop(1, rounds, unroll=True)
-    def _(i):
-        remote(root_tile, roots.at[i], ROOT, (lax.rem(o + l + locals_ * i, owners), l)).start()
-
-    @pl.when(jnp.logical_not(middle & rising))
-    def _():
-        pass_up()
-
-    @pl.when(jnp.logical_not(middle & jnp.logical_not(rising)))
-    def _():
-        pass_down()
 
     @pl.loop(1, locals_, unroll=True)
     def _(d):
@@ -337,6 +298,46 @@
         block = topw.at[pl.ds(l, 1)]
         remote(block, block, TOPW, peer).start()
 
+    edge = REACH * LEAF
+    width = leaves * LEAF
+    remote(vec_b.at[:, pl.ds(width - edge, edge)], halo.at[0], HALO, right_id).start()
+    remote(vec_b.at[:, pl.ds(0, edge)], halo.at[1], HALO2, left_id).start()
+
+    @pl.when(middle & rising)
+    def _():
+        pass_up()
+
+    @pl.when(middle & jnp.logical_not(rising))
+    def _():
+        pass_down()
+
+    received(part.at[pl.ds(0, locals_ - 1)], PART)
+    root = part[0]
+    for other in range(1, locals_):
+        root = root + part[other]
+    root_tile[...] = root.astype(jnp.bfloat16)
+    pl.semaphore_wait(known, 2)
+
+    @pl.when(l == 0)
+    def _():
+        roots[0] = root_tile[...]
+
+    @pl.when(l != 0)
+    def _():
+        remote(root_tile, roots.at[0], ROOT, (lax.rem(o + l, owners), l)).start()
+
+    @pl.loop(1, rounds, unroll=True)
+    def _(i):
+        remote(root_tile, roots.at[i], ROOT, (lax.rem(o + l + locals_ * i, owners), l)).start()
+
+    @pl.when(jnp.logical_not(middle & rising))
+    def _():
+        pass_up()
+
+    @pl.when(jnp.logical_not(middle & jnp.logical_not(rising)))
+    def _():
+        pass_down()
+
     def to_scalars(rows, sem):
         copy = pltpu.make_async_copy(req.at[rows], req_s.at[rows], sem)
         copy.start()
@@ -375,27 +376,33 @@
     column = lax.broadcasted_iota(jnp.int32, (1, NV, members * NV), 2)
     row = lax.broadcasted_iota(jnp.int32, (1, NV, members * NV), 1)
     member_of = jnp.where(lax.rem(column, NV) == row, column // NV, -1).astype(jnp.float32)
-    received(req.at[pl.ds(0, below_rows + above_rows)], PASSED)
-    passed = req[near_rows:owners].astype(jnp.float32)
-    at = lax.broadcasted_iota(jnp.int32, passed.shape, 2)
-    ones = [
-        (jnp.sum(jnp.where(at == o + half, passed, 0.0), axis=2, keepdims=True) == member_of).astype(jnp.float32)
-        for half in (0, HALF)
-    ]
-    rows = (owners - near_rows) * NV
-    both = jnp.concatenate([one.reshape(rows, members * NV) for one in ones], axis=0).astype(jnp.bfloat16)
-    both = dot(both, skel_rows[...])
-    wide_low = lax.broadcasted_iota(jnp.int32, (rows, WIDE), 1) < HALF
-    both = jnp.where(wide_low, both[:rows], both[rows:])
-    far_send[near_rows:owners] = both.reshape(owners - near_rows, NV, WIDE).astype(jnp.bfloat16)
+
+    def choose_passed(begin, count, kind):
+        received(req.at[pl.ds(0, count)], kind)
+        passed = req[begin : begin + count].astype(jnp.float32)
+        at = lax.broadcasted_iota(jnp.int32, passed.shape, 2)
+        ones = [
+            (jnp.sum(jnp.where(at == o + half, passed, 0.0), axis=2, keepdims=True) == member_of).astype(jnp.float32)
+            for half in (0, HALF)
+        ]
+        rows = count * NV
+        both = jnp.concatenate([one.reshape(rows, members * NV) for one in ones], axis=0).astype(jnp.bfloat16)
+        both = dot(both, skel_rows[...])
+        wide_low = lax.broadcasted_iota(jnp.int32, (rows, WIDE), 1) < HALF
+        both = jnp.where(wide_low, both[:rows], both[rows:])
+        far_send[begin : begin + count] = both.reshape(count, NV, WIDE).astype(jnp.bfloat16)
 
     def answer_below():
+        choose_passed(near_rows, below_rows, PASSED)
+
         @pl.loop(0, below_rows, unroll=True)
         def _(i):
             j = below_rows - 1 - i
             answer(near_rows + j, owner_at(-reach - 1 - j // PLANE, lax.rem(j, PLANE)))
 
     def answer_above():
+        choose_passed(near_rows + below_rows, above_rows, PASSED_DOWN)
+
         @pl.loop(0, above_rows, unroll=True)
         def _(i):
             j = above_rows - 1 - i
@@ -515,10 +522,9 @@
         return jnp.where(f < count_s[t], tile, 0.0)
 
     for g in range(clusters // 4):
-        acc = jnp.zeros((4 * NV, RANK), jnp.float32)
-        for f in range(slots):
-            lhs = quad([picked(4 * g + t, f) for t in range(4)])
-            acc = acc + dot_t(lhs, far_b[f, :, g * QUAD : (g + 1) * QUAD])
+        lhs = jnp.concatenate([quad([picked(4 * g + t, f) for t in range(4)]) for f in range(slots)], axis=1)
+        rhs = jnp.concatenate([far_b[f, :, g * QUAD : (g + 1) * QUAD] for f in range(slots)], axis=1)
+        acc = dot_t(lhs, rhs)
         for t in range(4):
             at = 4 * g + t
             cluster_out = acc[t * NV : (t + 1) * NV] + downward[:, at * RANK : (at + 1) * RANK]
@@ -531,7 +537,9 @@
     sent(skel.at[pl.ds(0, clusters * (locals_ - 1))], SKEL)
     sent(part.at[pl.ds(0, locals_ - 1)], PART)
     sent(req.at[pl.ds(0, near_rows - 1)], REST)
-    sent(req.at[pl.ds(0, below_rows + above_rows)], PASSED)
+    sent(req.at[pl.ds(0, below_rows)], PASSED)
+    if above_rows:
+        sent(req.at[pl.ds(0, above_rows)], PASSED_DOWN)
     sent(tops.at[pl.ds(0, locals_ - 1)], TOPS)
     sent(topw.at[pl.ds(0, locals_ - 1)], TOPW)
     sent(halo.at[0], HALO)

time: 35.9 us -> 35.8 us (level)
  no operation moved by 1% of the time
where the time goes in v5:
time: 35.8 us; the launch traced here: 35.6 us
  Pallas kernels  35 us (98%)
  local copies, waits for them, and re-layouts  0.62 us (2%)
    pallas_call x1, Pallas kernels, per_device(): pl.pallas_call(functools.partial(kernel, owners, locals_), out_shape=pltp...  35 us

profile of v5, /device:TPU:2, one launch (start us, length us, event | category | flops | bytes accessed | tf_op | source)
XLA Modules:
  0.0 35.6 jit_solution(570035154464492137)
XLA Ops:
  0.0 35.0 %shard_map.118 = bf16[8,2048]{1,0:T(8,128)(2,1)S(1)} custom-call(bf16[8,2048]{1,0:T(8,128)(2,1)} %vec.1, bf16[64,2048]{1,0:T(8,128)(2,1)} %basis.1, bf16[4,64,2048]{2,1,0:T(8,128)(2,1)} %near.1, bf16[64,2048]{1,0:T(8,128)(2,1)} %up.1, bf16[8,64,512]{2,1,0:T(8,128)(2,1)} %far.1, bf16[64,512]{1,0:T(8,128)(2,1)} %root_t.1, bf16[2,64,64]{2,1,0:T(8,128)(2,1)} %top_b.1, ...), custom_call_target="tpu_custom_call" | custom-call | tf_op jit(solution)/shard_map/pallas_call | solution.py:582
  35.0 0.6 %copy.14 = bf16[8,2048]{1,0:T(8,128)(2,1)} copy(bf16[8,2048]{1,0:T(8,128)(2,1)S(1)} %shard_map.118) | data formatting | bytes 65536
